TPU v7x, 32 devices: a whole 2x2x4 slice. The times are simulated.
32 devices in a mesh: dp: 16 (over z, y, x), tensor: 2 (over core).
Axes of the slice: x: 2, y: 2, z: 4, core: 2. Of those that a mesh axis runs over, the one named last changes fastest.
Arguments:
- tokens: bfloat16 [16, 1024, 768], P('dp', 'tensor'), may hold values from -6 to 6
- temb: bfloat16 [16, 768], P('dp'), may hold values from -6 to 6
- lengths: int32 [16], P('dp'), may hold values from 128 to 1024, as said below
- w_mod: bfloat16 [768, 4608], P('dp'), may hold values from -0.109375 to 0.109375
- b_mod: bfloat16 [4608], replicated, may hold values from -1.796875 to 1.796875
- gain_attn: bfloat16 [768], replicated, may hold values from 0.25 to 1.75
- query_key_value_weight: bfloat16 [768, 3, 768], P(None, None, 'tensor'), may hold values from -0.21875 to 0.21875
- b_qkv: bfloat16 [3, 768], P(None, 'tensor'), may hold values from -1.796875 to 1.796875
- attention_output_weight: bfloat16 [768, 768], P('tensor'), may hold values from -1.25 to 1.25
- gain_mlp: bfloat16 [768], replicated, may hold values from 0.25 to 1.75
- up_weight: bfloat16 [768, 3072], P(None, 'tensor'), may hold values from -0.21875 to 0.21875
- b_up: bfloat16 [3072], P('tensor'), may hold values from -3 to 3
- down_weight: bfloat16 [3072, 768], P('tensor'), may hold values from -0.21875 to 0.21875
- b_down: bfloat16 [768], replicated, may hold values from -1.796875 to 1.796875
- cotangent: bfloat16 [16, 1024, 768], P('dp', 'tensor'), may hold values from -6 to 6
Outputs:
- output: bfloat16 [16, 1024, 768], P('dp', 'tensor')
- grad_tokens: bfloat16 [16, 1024, 768], P('dp', 'tensor')
- grad_temb: float32 [16, 768], P('dp')
- grad_w_mod: float32 [768, 4608], P('dp')
- grad_b_mod: float32 [4608], replicated
- grad_gain_attn: float32 [768], replicated
- grad_w_qkv: float32 [768, 3, 768], P(None, None, 'tensor')
- grad_b_qkv: float32 [3, 768], P(None, 'tensor')
- grad_w_out: float32 [768, 768], P('tensor')
- grad_gain_mlp: float32 [768], replicated
- up_weight_gradient: float32 [768, 3072], P(None, 'tensor')
- grad_b_up: float32 [3072], P('tensor')
- grad_w_down: float32 [3072, 768], P('tensor')
- grad_b_down: float32 [768], replicated
Inputs may be any that keep to these rules, and one draw needn't show every extreme that they name: `lengths`: each sequence's count of valid tokens, more of them near the low end; one sequence in all has exactly 1024.
All inputs are finite; a program needn't handle non-finite values.
Results may differ from a plain program's by a relative error of at most 0.018.
Values may be sent and summed in bfloat16 or wider, within the bound.
No kernel may reach another device: no remote copies, remote signals or barrier semaphores. Data moves between devices by JAX's collectives and lax.ppermute only.
A program may use at most 192 MiB of HBM per device.

v0:
```python
from math import log, pi, sqrt

import jax
import jax.numpy as jnp
from jax import lax
from jax.experimental import pallas as pl
from jax.experimental.pallas import tpu as pltpu
from jax.sharding import PartitionSpec as P

HEAD_DIM = 64
PAIR = 2 * HEAD_DIM
F32 = jnp.float32
BF16 = jnp.bfloat16
NN = ((1,), (0,))
NT = ((1,), (1,))
TN = ((0,), (0,))
SAFE = 90.0
LN2 = log(2.0)
MIB = 1024 * 1024
VM = pl.BlockSpec(memory_space=pltpu.VMEM)
SM = pl.BlockSpec(memory_space=pltpu.SMEM)


def dot(left, right, dims=NN):
    return lax.dot_general(left, right, (dims, ((), ())), preferred_element_type=F32)


def call(
    body, grid, in_specs, out_specs, out_shape, args, scratch=(), flops=0, moved=0, deps=(), room=6, aliases=None
):
    count = len(in_specs)
    extra = len(deps)
    args = [
        near_core(arg) if spec is VM and arg.size >= 1 << 16 else arg for spec, arg in zip(in_specs, args)
    ]

    def wrapped(*refs):
        body(*refs[:count], *refs[count + extra :])

    return pl.pallas_call(
        wrapped,
        grid=grid,
        in_specs=list(in_specs) + [pl.BlockSpec(memory_space=pl.ANY)] * extra,
        out_specs=out_specs,
        out_shape=out_shape,
        scratch_shapes=list(scratch),
        input_output_aliases=aliases or {},
        compiler_params=pltpu.CompilerParams(
            vmem_limit_bytes=room * MIB, dimension_semantics=("arbitrary",) * len(grid)
        ),
        cost_estimate=pl.CostEstimate(flops=0, bytes_accessed=0, transcendentals=0),
    )(*args, *deps)


def whole(shape):
    return pl.BlockSpec(shape, lambda *_: (0,) * len(shape))


def shape_of(shape, kind):
    return pltpu.VMEM(shape, kind)


def near_core(value):
    return pltpu.with_memory_space_constraint(value, pltpu.VMEM)


def far_core(value):
    return pltpu.with_memory_space_constraint(value, pltpu.HBM)


def norm_parts(field):
    centred = field - jnp.mean(field, axis=-1, keepdims=True)
    inverse = lax.rsqrt(jnp.mean(centred * centred, axis=-1, keepdims=True) + 1e-05)
    return (centred * inverse, inverse)


def norm_back(upstream, normed, inverse):
    return inverse * (
        upstream
        - jnp.mean(upstream, axis=-1, keepdims=True)
        - normed * jnp.mean(upstream * normed, axis=-1, keepdims=True)
    )


def gelu_parts(hidden):
    scale = sqrt(2.0 / pi)
    square = hidden * hidden
    bent = jnp.tanh(hidden * (scale + (scale * 0.044715) * square))
    upper = 0.5 + 0.5 * bent
    slope = upper + (hidden * (0.5 - 0.5 * bent * bent)) * (scale + (3 * 0.044715 * scale) * square)
    return (hidden * upper, slope)


def turn_lanes(field):
    lane = lax.broadcasted_iota(jnp.int32, field.shape, 1)
    up = pltpu.roll(field, PAIR - HEAD_DIM // 2, 1)
    down = pltpu.roll(field, HEAD_DIM // 2, 1)
    return jnp.where((lane & (HEAD_DIM - 1)) < HEAD_DIM // 2, up, down)


def zero_other(field, h, axis):
    place = lax.broadcasted_iota(jnp.int32, field.shape, axis)
    return jnp.where((place >= HEAD_DIM) == (h == 1), field, jnp.zeros_like(field))


def total(field):
    return jnp.sum(field, axis=0, keepdims=True)


def both(near, far):
    return jnp.concatenate([near[...], far[...]], axis=0)


def project_call(near, far, weight, bias, cosine, sine):
    rows, width = near.shape
    half = weight.shape[2]

    def body(xn, xf, w, b, cos, sin, out):
        for i, x in enumerate((xn, xf)):
            here = slice(i * rows, (i + 1) * rows)
            for c in range(3):
                y = dot(x[...], w[c]) + b[c]
                if c == 2:
                    out[c, here] = y.astype(BF16)
                    continue
                for j in range(half // PAIR):
                    of = slice(j * PAIR, (j + 1) * PAIR)
                    u = y[:, of]
                    u = u * cos[here] + turn_lanes(u) * sin[here]
                    if c == 0:
                        u = u * (HEAD_DIM ** (-0.5) / LN2)
                    out[c, here, of] = u.astype(BF16)

    return call(
        body,
        (),
        [VM] * 6,
        VM,
        shape_of((3, 2 * rows, half), BF16),
        (near, far, weight, bias, cosine, sine),
        room=8,
    )


def attend_call(counts, qkv, weight):
    _, keys, half = qkv.shape
    rows = keys // 2
    pairs = half // PAIR
    width = weight.shape[1]

    def body(cnt, q_in, k_in, v_in, w, e_out, ot_out, inv_out, near_out, far_out, o_all):
        j = pl.program_id(0)
        k = k_in[0]
        v_t = v_in[0].T
        near_count, far_count = cnt[0], cnt[1]

        def run(masked, plain):
            for p in range(2):
                of = slice(p * rows, (p + 1) * rows)
                q_t = q_in[0, of].T
                for h in range(2):
                    hs = slice(h * HEAD_DIM, (h + 1) * HEAD_DIM)
                    s = dot(k, zero_other(q_t, h, 0))
                    if masked:
                        place = lax.broadcasted_iota(jnp.int32, (keys, rows), 0)
                        limit = jnp.where(place < rows, near_count, rows + far_count)
                        s = jnp.where(place < limit, s, -1e30)
                    if not plain:
                        s = s - jnp.max(s, axis=0, keepdims=True)
                    e = jnp.exp2(s)
                    inv = 1.0 / total(e)
                    e = e.astype(BF16)
                    e_out[0, h, p] = e
                    inv_out[0, h, :, of] = inv
                    ot_out[hs, of] = (dot(v_t[hs], e) * inv).astype(BF16)

        def norms(field):
            square = field.astype(F32) * field.astype(F32)
            return [
                jnp.max(jnp.sum(zero_other(square, h, 1), axis=1, keepdims=True)) for h in range(2)
            ]

        bound = 0.0
        for one, two in zip(norms(q_in[0]), norms(k)):
            bound = jnp.maximum(bound, one * two)
        plain = bound < SAFE * SAFE
        everything = near_count + far_count >= keys
        pl.when(plain & everything)(lambda: run(False, True))
        pl.when(plain & jnp.logical_not(everything))(lambda: run(True, True))
        pl.when(jnp.logical_not(plain))(lambda: run(True, False))
        o_all[j] = ot_out[...].T

        @pl.when(j == pairs - 1)
        def _():
            o = jnp.concatenate([o_all[i] for i in range(pairs)], axis=1)
            near_out[...] = dot(o[:rows], w[...])
            far_out[...] = dot(o[rows:], w[...]).astype(BF16)

    pick_pair = lambda c: pl.BlockSpec((1, keys, PAIR), lambda j: (c, 0, j))
    return call(
        body,
        (pairs,),
        [SM, pick_pair(0), pick_pair(1), pick_pair(2), whole((half, width))],
        [
            pl.BlockSpec((1, 2, 2, keys, rows), lambda j: (j, 0, 0, 0, 0)),
            pl.BlockSpec((PAIR, keys), lambda j: (j, 0)),
            pl.BlockSpec((1, 2, 1, keys), lambda j: (j, 0, 0, 0)),
            whole((rows, width)),
            whole((rows, width)),
        ],
        [
            pltpu.HBM((pairs, 2, 2, keys, rows), BF16),
            shape_of((half, keys), BF16),
            shape_of((pairs, 2, 1, keys), F32),
            shape_of((rows, width), F32),
            shape_of((rows, width), BF16),
        ],
        (counts, qkv, qkv, qkv, weight),
        [pltpu.VMEM((pairs, keys, PAIR), BF16)],
        flops=16 * keys * keys * half,
        moved=2 * keys * keys * half // HEAD_DIM,
        room=20,
    )


def middle_call(tokens, near, far, vecs):
    rows, width = tokens.shape

    def body(tok, nr, fr, vec, branch_out, fed_out):
        branch = nr[...] + fr[...].astype(F32)
        branch_out[...] = branch
        normed, _ = norm_parts(tok[...].astype(F32) + vec[2:3] * branch)
        fed_out[...] = (normed * vec[3:4] + vec[4:5]).astype(BF16)

    return call(
        body,
        (),
        [VM] * 4,
        [VM] * 2,
        [shape_of((rows, width), F32), shape_of((rows, width), BF16)],
        (tokens, near, far, vecs),
        moved=12 * rows * width,
    )


def mlp_call(first, units, bits, fed, far, g, g_far, up, down, bias, deps=()):
    rows, width = fed.shape
    tile = 256

    def body(bit, fed_in, far_in, g_in, gf_in, up_in, down_in, b_in, send, keep, act_out, dh_out, sums):
        def step(n, carry):
            here = pl.ds(pl.multiple_of(n * tile, tile), tile)
            there = pl.ds(pl.multiple_of(first + n * tile, tile), tile)
            up_w, down_w = up_in[:, there], down_in[there]
            for i, (x, gr) in enumerate(((fed_in, g_in), (far_in, gf_in))):
                of = slice(i * rows, (i + 1) * rows)
                active, slope = gelu_parts(dot(x[...], up_w) + b_in[:, there])
                act_out[of, here] = active.astype(BF16)
                dh_out[of, here] = (dot(gr[...], down_w, NT) * slope).astype(BF16)
            d_hidden = dh_out[:, here]
            down_part = dot(act_out[:, here], both(g_in, gf_in), TN).astype(BF16)
            up_part = dot(both(fed_in, far_in), d_hidden, TN).astype(BF16)
            sums[:, here] = total(d_hidden.astype(F32))

            @pl.when(bit[0] == 0)
            def _():
                keep[here, :] = down_part
                send[:, here] = up_part

            @pl.when(bit[0] != 0)
            def _():
                send[here, :] = down_part
                keep[:, here] = up_part

            return carry

        lax.fori_loop(0, units // tile, step, 0)

    return call(
        body,
        (),
        [SM] + [VM] * 7,
        [VM] * 5,
        [shape_of((width, units), BF16)] * 2
        + [shape_of((2 * rows, units), BF16)] * 2
        + [shape_of((1, units), F32)],
        (bits, fed, far, g, g_far, up, down, bias),
        deps=deps,
        room=12,
    )


def terms_call(parts, weight, dims, deps=()):
    keys, units = parts[0].shape
    rows = keys // 2
    width = weight.shape[0] if dims is NT else weight.shape[1]

    def body(*refs):
        ins, w, near, far = refs[:-3], refs[-3], refs[-2], refs[-1]
        for i, out in enumerate((near, far)):
            acc = 0.0
            for n, part in enumerate(ins):
                of = slice(n * units, (n + 1) * units)
                piece = w[:, of] if dims is NT else w[of]
                acc = acc + dot(part[i * rows : (i + 1) * rows], piece, dims)
            out[...] = acc.astype(out.dtype)

    return call(
        body,
        (),
        [VM] * (len(parts) + 1),
        [VM] * 2,
        [shape_of((rows, width), F32), shape_of((rows, width), BF16)],
        (*parts, weight),
        flops=2 * keys * width * units * len(parts),
        moved=8 * keys * width,
        deps=deps,
        room=8,
    )


def input_call(normed, vecs):
    rows, width = normed.shape

    def body(n, vec, out):
        out[...] = (n[...] * vec[0:1] + vec[1:2]).astype(BF16)

    return call(body, (), [VM, VM], VM, shape_of((rows, width), BF16), (normed, vecs))


def masked(cnt, field):
    place = lax.broadcasted_iota(jnp.int32, field.shape, 0)
    return jnp.where(place < cnt[0], field.astype(F32), 0.0)


def upstream_call(counts, cotangent, vecs):
    rows, width = cotangent.shape

    def body(cnt, cot, vec, g_out, sum_out):
        g = (masked(cnt, cot[...]) * vec[5:6]).astype(BF16)
        g_out[...] = g
        sum_out[...] = total(g.astype(F32))

    return call(
        body,
        (),
        [SM, VM, VM],
        [VM, VM],
        [shape_of((rows, width), BF16), shape_of((1, width), F32)],
        (counts, cotangent, vecs),
    )


def turn_call(counts, tokens, cotangent, branch, d_near, d_far, vecs, deps=()):
    rows, width = tokens.shape

    def body(cnt, tok, cot, br, dn, df, vec, dm_out, g_out, sum_out):
        normed, inverse = norm_parts(tok[...].astype(F32) + vec[2:3] * br[...])
        d_in = dn[...] + df[...].astype(F32)
        d_middle = masked(cnt, cot[...]) + norm_back(d_in * vec[3:4], normed, inverse)
        g_out[...] = (d_middle * vec[2:3]).astype(BF16)
        dm_out[...] = d_middle
        sum_out[0:1] = total(d_middle * br[...])
        sum_out[1:2] = total(d_in)
        sum_out[2:3] = total(d_in * normed)
        sum_out[3:8] = jnp.zeros((5, width), F32)

    return call(
        body,
        (),
        [SM] + [VM] * 6,
        [VM] * 3,
        [shape_of((rows, width), F32), shape_of((rows, width), BF16), shape_of((8, width), F32)],
        (counts, tokens, cotangent, branch, d_near, d_far, vecs),
        deps=deps,
    )


def finish_call(counts, tokens, cotangent, branch, b_near, b_far, vecs, deps=()):
    rows, width = tokens.shape

    def body(cnt, tok, cot, br, bn, bf, vec, y_out, sum_out):
        middle = tok[...].astype(F32) + vec[2:3] * br[...]
        mlp_branch = bn[...] + bf[...].astype(F32) + vec[6:7]
        y_out[...] = masked(cnt, middle + vec[5:6] * mlp_branch).astype(BF16)
        sum_out[0:1] = total(masked(cnt, cot[...]) * mlp_branch)
        sum_out[1:8] = jnp.zeros((7, width), F32)

    return call(
        body,
        (),
        [SM] + [VM] * 6,
        [VM] * 2,
        [pltpu.HBM((rows, width), BF16), shape_of((8, width), F32)],
        (counts, tokens, cotangent, branch, b_near, b_far, vecs),
        deps=deps,
    )


def turn_out_call(near, far, weight, o_t, deps=()):
    rows, width = near.shape
    half = weight.shape[0]

    def body(gn, gf, w, ot, d_out, w_out):
        g = jnp.concatenate([gn[...], gf[...]], axis=0)
        d_out[...] = dot(w[...], g, NT).astype(BF16)
        grad = dot(ot[...], g).astype(BF16)
        w_out[0:half] = grad[:, :half]
        w_out[half:] = grad[:, half:]

    return call(
        body,
        (),
        [VM] * 4,
        [VM] * 2,
        [shape_of((half, 2 * rows), BF16), shape_of((width, half), BF16)],
        (near, far, weight, o_t),
        flops=8 * rows * width * half,
        moved=6 * rows * width,
        deps=deps,
    )


def attend_back_call(j, qkv, e, o_t, inv, d_t, cosine, sine, near, far, deps=()):
    _, keys, half = qkv.shape
    rows = keys // 2
    width = near.shape[1]
    quarter = HEAD_DIM // 2

    def body(qkv_in, e_hbm, ot_all, inv_in, d_all, cos, sin, xn, xf, grad_out, d_out, sums, e_in, sems):
        lanes = slice(j * PAIR, (j + 1) * PAIR)
        ot_in, d_in = ot_all.at[lanes], d_all.at[lanes]

        def copy(p, h):
            n = 2 * p + h
            return pltpu.make_async_copy(e_hbm.at[j, h, p], e_in.at[n], sems.at[n])

        for p in range(2):
            for h in range(2):
                copy(p, h).start()
        k_t = qkv_in[1, :, lanes].T
        v = qkv_in[2, :, lanes]
        cos_t = cos[...].T[:quarter]
        sin_t = sin[...].T[quarter : 2 * quarter]
        d_k = d_v = 0.0
        d_q = []
        for p in range(2):
            of = slice(p * rows, (p + 1) * rows)
            scaled = []
            for h in range(2):
                hs = slice(h * HEAD_DIM, (h + 1) * HEAD_DIM)
                scaled.append((d_in[hs, of].astype(F32) * inv_in[j, h, :, of]).astype(BF16))
            d_t = jnp.concatenate(scaled, axis=0)
            d = d_t.T
            q = qkv_in[0, of, lanes]
            turned = []
            for h in range(2):
                hs = slice(h * HEAD_DIM, (h + 1) * HEAD_DIM)
                delta = total(d_t[hs].astype(F32) * ot_in[hs, of].astype(F32))
                d_p = dot(v, zero_other(d_t, h, 0))
                copy(p, h).wait()
                weight = e_in[2 * p + h]
                d_s = (weight.astype(F32) * (d_p - delta)).astype(BF16)
                d_v = d_v + dot(weight, zero_other(d, h, 1))
                d_k = d_k + dot(d_s, zero_other(q, h, 1))
                t = dot(k_t[hs], d_s) * HEAD_DIM ** (-0.5)
                one, two = t[:quarter], t[quarter:]
                turned.append((one * cos_t[:, of] + two * sin_t[:, of]).astype(BF16))
                turned.append((two * cos_t[:, of] - one * sin_t[:, of]).astype(BF16))
            d_q.append(jnp.concatenate(turned, axis=0).T)
        u = d_k * LN2
        d_k = (u * cos[...] - turn_lanes(u) * sin[...]).astype(BF16)
        every = jnp.concatenate([jnp.concatenate(d_q, axis=0), d_k, d_v.astype(BF16)], axis=1)
        d_out[...] = every
        grad_out[...] = dot(both(xn, xf), every, TN).astype(BF16)
        sums[...] = total(every.astype(F32))

    return call(
        body,
        (),
        [VM, pl.BlockSpec(memory_space=pltpu.HBM)] + [VM] * 7,
        [VM] * 3,
        [
            shape_of((width, 3 * PAIR), BF16),
            shape_of((keys, 3 * PAIR), BF16),
            shape_of((1, 3 * PAIR), F32),
        ],
        (qkv, far_core(e), o_t, inv, d_t, cosine, sine, near, far),
        [pltpu.VMEM((4, keys, rows), BF16), pltpu.SemaphoreType.DMA((4,))],
        flops=32 * keys * keys * PAIR,
        moved=4 * keys * keys,
        deps=deps,
        room=14,
    )


def input_terms_call(parts, weight, deps=()):
    keys = parts[0].shape[0]
    rows = keys // 2
    _, width, half = weight.shape

    def body(*refs):
        ins, w, near, far = refs[:-3], refs[-3], refs[-2], refs[-1]
        for i, out in enumerate((near, far)):
            acc = 0.0
            for c in range(3):
                of = slice(c * PAIR, (c + 1) * PAIR)
                d = jnp.concatenate([part[i * rows : (i + 1) * rows, of] for part in ins], axis=1)
                acc = acc + dot(d, w[c], NT)
            out[...] = acc.astype(out.dtype)

    return call(
        body,
        (),
        [VM] * (len(parts) + 1),
        [VM] * 2,
        [shape_of((rows, width), F32), shape_of((rows, width), BF16)],
        (*parts, weight),
        flops=6 * keys * width * half,
        moved=8 * keys * width,
        deps=deps,
        room=8,
    )


def end_call(tokens, d_middle, near, far, vecs, deps=()):
    rows, width = tokens.shape

    def body(tok, dm, dn, df, vec, grad_out, sum_out):
        normed, inverse = norm_parts(tok[...].astype(F32))
        d_in = dn[...] + df[...].astype(F32)
        grad_out[...] = (dm[...] + norm_back(d_in * vec[0:1], normed, inverse)).astype(BF16)
        sum_out[0:1] = total(d_in)
        sum_out[1:2] = total(d_in * normed)
        sum_out[2:8] = jnp.zeros((6, width), F32)

    return call(
        body,
        (),
        [VM] * 5,
        [VM] * 2,
        [pltpu.HBM((rows, width), BF16), shape_of((8, width), F32)],
        (tokens, d_middle, near, far, vecs),
        moved=16 * rows * width,
        deps=deps,
    )


def swap(value):
    return lax.ppermute(value, "tensor", [(0, 1), (1, 0)])


def bit_swap(value, bit, order_by_core):
    pairs = []
    for place in range(lax.axis_size("dp")):
        for core in range(2):
            use = bit ^ core if order_by_core else bit
            pairs.append((place * 2 + core, (place ^ (1 << use)) * 2 + core))
    return lax.ppermute(value, ("dp", "tensor"), pairs)


def pick(value, index):
    return lax.dynamic_index_in_dim(value, index, 0, keepdims=False)


def join(mine, other, index):
    return jnp.where(index == 0, jnp.stack([mine, other]), jnp.stack([other, mine]))


def bit_count():
    return lax.axis_size("dp").bit_length() - 1


def pack_call(blocks, bit, deps=()):
    width, size = blocks[0].shape

    def body(b, one, two, three, four, send, keep):
        def put(low, high):
            low[:, :size], low[:, size:] = one[...], two[...]
            high[:, :size], high[:, size:] = three[...], four[...]

        pl.when(b[0] == 0)(lambda: put(keep, send))
        pl.when(b[0] != 0)(lambda: put(send, keep))

    return call(
        body,
        (),
        [SM] + [VM] * 4,
        [VM, VM],
        [shape_of((width, 2 * size), BF16)] * 2,
        (bit, *blocks),
        deps=deps,
    )


def shared_call(end_sums, turn_sums, out_sums, down_sums, vecs, deps=()):
    width = vecs.shape[1]

    def body(ends, turn, out, down, vec, rows):
        rows[0:1] = ends[0:1]
        rows[1:2] = ends[1:2] * vec[7:8]
        rows[2:4] = turn[0:2]
        rows[4:5] = turn[2:3] * vec[8:9]
        rows[5:6] = out[0:1]
        rows[6:7] = ends[1:2] * vec[9:10]
        rows[7:8] = turn[2:3] * vec[10:11]
        rows[8:9] = down[...]
        rows[9:16] = jnp.zeros((7, width), F32)

    return call(
        body,
        (),
        [VM] * 5,
        VM,
        shape_of((16, width), F32),
        (end_sums, turn_sums, out_sums, down_sums, vecs),
        deps=deps,
    )


def small_call(mine, other, b_up_sums, b_qkv_sums, deps=()):
    width = mine.shape[1]
    half = width // 2

    def body(one, two, up_0, up_1, qkv_0, qkv_1, qkv_2, rows):
        rows[0:16] = (one[...] + two[...]).astype(BF16)
        extra = jnp.concatenate(
            [
                up_0[...],
                up_1[...],
                jnp.concatenate([qkv_0[...], qkv_1[...]], axis=1),
                jnp.concatenate([qkv_2[...], jnp.zeros((1, half), F32)], axis=1),
                jnp.zeros((12, width), F32),
            ],
            axis=0,
        )
        rows[16:32] = extra.astype(BF16)

    return call(
        body,
        (),
        [VM] * 7,
        VM,
        shape_of((32, width), BF16),
        (mine, other, *b_up_sums, *b_qkv_sums),
        deps=deps,
    )


def append_call(mine, other, deps=()):
    rows, width = mine.shape

    def body(one, two, out):
        out[:rows] = one[...]
        out[rows:] = two[...]

    return call(
        body, (), [VM, VM], VM, shape_of((2 * rows, width), BF16), (mine, other), deps=deps
    )


def split_add(mine, other, bit, deps=()):
    rows, width = mine.shape

    def body(b, one, two, send, keep):
        field = (one[...].astype(F32) + two[...].astype(F32)).astype(BF16)
        low, high = field[: rows // 2], field[rows // 2 :]

        @pl.when(b[0] == 0)
        def _():
            keep[...] = low
            send[...] = high

        @pl.when(b[0] != 0)
        def _():
            send[...] = low
            keep[...] = high

    return call(
        body,
        (),
        [SM, VM, VM],
        [VM, VM],
        [shape_of((rows // 2, width), BF16)] * 2,
        (bit, mine, other),
        moved=6 * rows * width,
        deps=deps,
    )


def plain_add(mine, other, deps=()):
    def body(one, two, out):
        out[...] = (one[...].astype(F32) + two[...].astype(F32)).astype(BF16)

    return call(
        body, (), [VM, VM], VM, shape_of(mine.shape, BF16), (mine, other), moved=6 * mine.size, deps=deps
    )


def stack_halves(mine, other, bit, deps=()):
    rows, width = mine.shape

    def body(b, one, two, out):
        out[pl.ds(pl.multiple_of(b[0] * rows, rows), rows)] = one[...]
        out[pl.ds(pl.multiple_of((1 - b[0]) * rows, rows), rows)] = two[...]

    return call(
        body,
        (),
        [SM, VM, VM],
        VM,
        shape_of((2 * rows, width), BF16),
        (bit, mine, other),
        moved=8 * mine.size,
        deps=deps,
    )


def unpack_call(mine, other, bit, before, units, at, deps=()):
    width = mine.shape[0]
    size = mine.shape[1]

    def body(b, one, two, *rest):
        down_out, up_out = rest[-2:]

        @pl.when(b[0] == 0)
        def _():
            down_out[...] = one[...].astype(F32)
            up_out[...] = two[...].astype(F32)

        @pl.when(b[0] != 0)
        def _():
            down_out[...] = two[...].astype(F32)
            up_out[...] = one[...].astype(F32)

    extra = [pl.BlockSpec(memory_space=pl.ANY)] * len(before)
    return call(
        body,
        (1,),
        [SM, whole(mine.shape), whole(mine.shape)] + extra,
        [
            pl.BlockSpec((size, width), lambda i: (at, 0)),
            pl.BlockSpec((width, size), lambda i: (0, at)),
        ],
        [pltpu.HBM((units, width), F32), pltpu.HBM((width, units), F32)],
        (bit, mine, other) + tuple(far_core(x) for x in before),
        moved=12 * mine.size,
        deps=deps,
        aliases={3: 0, 4: 1} if before else None,
        room=16,
    )


def unpack_last_call(mine, other, bit, deps=()):
    width, size = mine.shape
    half = size // 2

    def body(b, one, two, qkv_out, out_out):
        def put(low, high):
            for j, block in enumerate((low[:, :half], low[:, half:], high[:, :half])):
                for c in range(3):
                    qkv_out[c, :, j * PAIR : (j + 1) * PAIR] = block[:, c * PAIR : (c + 1) * PAIR].astype(F32)
            out_out[:, :half] = high[:half, half:].astype(F32)
            out_out[:, half:] = high[half:, half:].astype(F32)

        pl.when(b[0] == 0)(lambda: put(one, two))
        pl.when(b[0] != 0)(lambda: put(two, one))

    return call(
        body,
        (),
        [SM, VM, VM],
        [VM, VM],
        [pltpu.HBM((3, width, half), F32), pltpu.HBM((half, width), F32)],
        (bit, mine, other),
        moved=12 * mine.size,
        deps=deps,
    )


def reduce_steps(send, keep, bits, halve):
    first, second, third = bits
    other = bit_swap(send, 0, True)
    deps = yield other
    send, keep = split_add(keep, other, second, deps)
    other = bit_swap(send, 1, True)
    deps = yield send, other
    if halve:
        send, keep = split_add(keep, other, third, deps)
        other = bit_swap(send, 2, False)
        deps = yield send, other
        mine = plain_add(keep, other, deps)
    else:
        mine = plain_add(keep, other, deps)
        other = bit_swap(mine, 2, False)
        deps = yield mine, other
        mine = plain_add(mine, other, deps)
    for bit in range(3, bit_count()):
        other = bit_swap(mine, bit, False)
        deps = yield mine, other
        mine = plain_add(mine, other, deps)
    if halve:
        other = bit_swap(mine, 2, False)
        deps = yield mine, other
        mine = stack_halves(mine, other, third, deps)
    other = bit_swap(mine, 1, True)
    deps = yield mine, other
    mine = stack_halves(mine, other, second, deps)
    yield mine, (mine, bit_swap(mine, 0, True))


class Gather:
    def __init__(self, value, line):
        self.line = line
        self.value = value
        self.bit = 0
        self.other = bit_swap(value, 0, False)

    def go(self):
        if self.bit < bit_count():
            self.value = append_call(self.value, self.other, self.line.last)
            self.line.after(self.value)
            self.bit += 1
            if self.bit < bit_count():
                self.other = bit_swap(self.value, self.bit, False)

    def all(self):
        while self.bit < bit_count():
            self.go()
        return self.value


def tree_sum(value):
    while value.shape[0] > 1:
        value = value.reshape((-1, 2) + value.shape[1:])
        value = value[:, 0] + value[:, 1]
    return value[0]


class Line:
    def __init__(self):
        self.last = ()

    def after(self, value):
        self.last = (value,)


class Group:
    def __init__(self, name, send, keep, bits, line, halve=True):
        self.line = line
        self.name = name
        self.steps = reduce_steps(send, keep, bits, halve)
        self.done = False
        with jax.named_scope(name):
            self.waiting = next(self.steps)

    def go(self):
        if not self.done:
            with jax.named_scope(self.name):
                mine, self.waiting = self.steps.send(self.line.last)
            self.line.after(mine)
            self.done = isinstance(self.waiting, tuple)

    def halves(self):
        while not self.done:
            self.go()
        return self.waiting


def shards(
    tokens,
    temb,
    lengths,
    w_mod,
    b_mod,
    gain_attn,
    query_key_value_weight,
    b_qkv,
    attention_output_weight,
    gain_mlp,
    up_weight,
    b_up,
    down_weight,
    b_down,
    cotangent,
):
    tokens, cotangent, length = tokens[0], cotangent[0], lengths[0]
    rows, width = tokens.shape
    core = lax.axis_index("tensor")
    place = lax.axis_index("dp")
    bits = [
        jnp.reshape((place >> b) & 1, (1,)).astype(jnp.int32) for b in (core, 1 - core, jnp.int32(2))
    ]
    half = width // 2
    start = core * rows
    counts = jnp.clip(jnp.stack([length - start, length - (rows - start)]), 0, rows)

    qkv_weight = jnp.swapaxes(query_key_value_weight, 0, 1)
    qkv_bias = b_qkv.reshape(3, 1, half).astype(F32)
    up_bias = b_up.reshape(1, -1).astype(F32)
    quarter = HEAD_DIM // 2
    lane = lax.iota(jnp.int32, PAIR)
    frequency = 10000.0 ** (-(lane & (quarter - 1)).astype(F32) / quarter)
    sign = jnp.where((lane & quarter) == 0, -1.0, 1.0)
    order = lax.iota(jnp.int32, rows)
    places = jnp.concatenate([start + order, (rows - start) + order]).astype(F32)
    angles = places[:, None] * frequency[None, :]
    cosine, sine = jnp.cos(angles), jnp.sin(angles) * sign[None, :]
    normed_attn, _ = norm_parts(tokens.astype(F32))

    embed_part = lax.all_to_all(temb, "dp", split_axis=1, concat_axis=0, tiled=True)
    mod_terms = jnp.dot(embed_part, w_mod, preferred_element_type=F32)
    mod_terms = lax.all_to_all(mod_terms, "dp", split_axis=0, concat_axis=0, tiled=True)
    mod_terms, cosine, sine, normed_attn, qkv_bias, up_bias = lax.optimization_barrier(
        (mod_terms, cosine, sine, normed_attn, qkv_bias, up_bias)
    )
    modulation = jnp.sum(mod_terms, axis=0) + b_mod.astype(F32)
    shift_attn, scale_attn, gate_attn, shift_mlp, scale_mlp, gate_mlp = modulation.reshape(6, width)
    gain_attn = gain_attn.astype(F32)
    gain_mlp = gain_mlp.astype(F32)
    vecs = jnp.stack(
        [
            gain_attn * (1.0 + scale_attn),
            shift_attn,
            gate_attn,
            gain_mlp * (1.0 + scale_mlp),
            shift_mlp,
            gate_mlp,
            b_down.astype(F32),
            gain_attn,
            gain_mlp,
            1.0 + scale_attn,
            1.0 + scale_mlp,
        ]
    )

    attn_in = input_call(normed_attn, vecs)
    attn_in_far = swap(attn_in)
    qkv = project_call(attn_in, attn_in_far, qkv_weight, qkv_bias, cosine, sine)
    g_mlp, down_sums = upstream_call(counts, cotangent, vecs)
    g_mlp_far = swap(g_mlp)
    e, o_t, inv, branch_near, branch_far = attend_call(counts, qkv, attention_output_weight)
    attn_branch, fed = middle_call(tokens, branch_near, swap(branch_far), vecs)
    fed_far = swap(fed)
    units = up_weight.shape[1]
    size = units // 2
    line = Line()
    actives, d_hiddens, b_up_sums, groups = [], [], [], []
    for part in range(2):
        send, keep, active, d_hidden, b_up_sum = mlp_call(
            part * size, size, bits[0], fed, fed_far, g_mlp, g_mlp_far, up_weight, down_weight, up_bias, line.last
        )
        line.after(send)
        groups.append(Group(("mlp_first", "mlp_second")[part], send, keep, bits, line))
        actives.append(active)
        d_hiddens.append(d_hidden)
        b_up_sums.append(b_up_sum)
    one, two = groups
    d_near, d_far = terms_call(d_hiddens, up_weight, NT, line.last)
    line.after(d_far)
    b_near, b_far = terms_call(actives, down_weight, NN, line.last)
    line.after(b_far)
    d_middle, g_attn, turn_sums = turn_call(
        counts, tokens, cotangent, attn_branch, d_near, swap(d_far), vecs, line.last
    )
    line.after(g_attn)
    b_swapped = swap(b_far)
    g_attn_far = swap(g_attn)
    one.go()
    d_t, grad_out = turn_out_call(g_attn, g_attn_far, attention_output_weight, o_t, line.last)
    line.after(d_t)
    grads, d_alls, b_qkv_sums = [], [], []
    for j in range(half // PAIR):
        grad, d_all, b_qkv_sum = attend_back_call(
            j, qkv, e, o_t, inv, d_t, cosine, sine, attn_in, attn_in_far, line.last
        )
        line.after(grad)
        grads.append(grad)
        d_alls.append(d_all)
        b_qkv_sums.append(b_qkv_sum)
        if j < 2:
            two.go()
            one.go()
    send, keep = pack_call(grads + [grad_out], bits[0], line.last)
    line.after(send)
    three = Group("projections", send, keep, bits, line)
    d_near, d_far = input_terms_call(d_alls, qkv_weight, line.last)
    line.after(d_far)
    output, out_sums = finish_call(
        counts, tokens, cotangent, attn_branch, b_near, b_swapped, vecs, line.last
    )
    line.after(output)
    two.go()
    one.go()
    three.go()
    grad_tokens, end_sums = end_call(tokens, d_middle, d_near, swap(d_far), vecs, line.last)
    line.after(grad_tokens)
    shared = shared_call(end_sums, turn_sums, out_sums, down_sums, vecs, line.last)
    line.after(shared)
    shared_far = swap(shared)
    two.go()
    one.go()
    three.go()
    small = small_call(shared, shared_far, b_up_sums, b_qkv_sums, line.last)
    line.after(small)
    gather = Gather(small, line)
    two.go()
    one.go()
    three.go()
    gather.go()
    two.go()
    three.go()
    gather.go()
    totals = unpack_call(*one.halves(), bits[0], (), units, 0, line.last)
    line.after(totals[0])
    three.go()
    gather.go()
    totals = unpack_call(*two.halves(), bits[0], totals, units, 1, line.last)
    line.after(totals[0])
    three.go()
    every = gather.all().reshape(-1, 32, width)
    grad_mod_all = every[:, :6].reshape(-1, 6 * width)
    embed_order = lax.iota(jnp.int32, every.shape[0]) ^ place
    embed_here = jnp.take(embed_part, embed_order, axis=0)
    grad_w_mod = dot(embed_here, grad_mod_all, TN)
    embed_terms = jnp.take(dot(grad_mod_all, w_mod, NT), embed_order, axis=0)
    grad_temb = lax.all_to_all(embed_terms, "dp", split_axis=0, concat_axis=1, tiled=True)
    sums = tree_sum(every.astype(F32))

    down_total, up_total = totals
    qkv_total, out_total = unpack_last_call(*three.halves(), bits[0], line.last)
    b_up_total = sums[16:18].reshape(-1)
    b_qkv_total = sums[18:20].reshape(-1)[: 9 * PAIR].reshape(3, 3, PAIR)
    return (
        output[None],
        grad_tokens[None],
        grad_temb,
        grad_w_mod,
        sums[:6].reshape(-1),
        sums[6],
        jnp.swapaxes(qkv_total, 0, 1),
        jnp.swapaxes(b_qkv_total, 0, 1).reshape(3, half),
        out_total,
        sums[7],
        up_total,
        b_up_total,
        down_total,
        sums[8],
    )


def solution(mesh):
    return jax.shard_map(
        shards,
        mesh=mesh,
        in_specs=(
            P("dp", "tensor", None),
            P("dp", None),
            P("dp"),
            P("dp", None),
            P(),
            P(),
            P(None, None, "tensor"),
            P(None, "tensor"),
            P("tensor", None),
            P(),
            P(None, "tensor"),
            P("tensor"),
            P("tensor", None),
            P(),
            P("dp", "tensor", None),
        ),
        out_specs=(
            P("dp", "tensor", None),
            P("dp", "tensor", None),
            P("dp", None),
            P("dp", None),
            P(),
            P(),
            P(None, None, "tensor"),
            P(None, "tensor"),
            P("tensor", None),
            P(),
            P(None, "tensor"),
            P("tensor"),
            P("tensor", None),
            P(),
        ),
        check_vma=False,
    )
```

profile of v0, /device:TPU:0, one launch (start us, length us, event | category | flops | bytes accessed | tf_op | source)
XLA Modules:
  0.0 292.7 jit_solution(9420433832628256972)
XLA Ops:
  2.1 8.3 %all-to-all-start = ((bf16[1,16,48]{2,0,1:T(2,128)(2,1)}), bf16[1,16,48]{2,0,1:T(2,128)(2,1)S(1)}, u32[]{:S(2)}, u32[]{:S(2)}) async-start(bf16[1,16,48]{2,0,1:T(2,128)(2,1)} %all_to_all.38), calls=%async_computation | async-start | bytes 16384 | tf_op jit(solution)/shard_map/all_to_all | solution.py:911
  13.4 4.3 %all-to-all-done = bf16[1,16,48]{2,0,1:T(2,128)(2,1)S(1)} async-done(((bf16[1,16,48]{2,0,1:T(2,128)(2,1)}), bf16[1,16,48]{2,0,1:T(2,128)(2,1)S(1)}, u32[]{:S(2)}, u32[]{:S(2)}) %all-to-all-start) | async-done | bytes 1568 | tf_op jit(solution)/shard_map/all_to_all | solution.py:911
  18.8 4.2 %all-to-all-start.1 = ((f32[16,1,4608]{2,1,0:T(1,128)}), f32[16,1,4608]{2,1,0:T(1,128)}, u32[]{:S(2)}, u32[]{:S(2)}) async-start(f32[16,1,4608]{2,1,0:T(1,128)} %copy.38), calls=%async_computation.1 | async-start | bytes 589824 | tf_op jit(solution)/shard_map/all_to_all | solution.py:913
  23.2 3.0 %fusion.4 = (f32[1024,128]{1,0:T(8,128)S(1)}, f32[1024,128]{1,0:T(8,128)}) fusion(f32[128]{0:T(128)S(1)} %get-tuple-element.169, f32[128]{0:T(128)S(1)} %get-tuple-element.170, f32[1024]{0:T(1024)S(1)} %add_convert_fusion), kind=kLoop, calls=%fused_computation.13 | loop fusion | flops 262144 | bytes 1053696 | tf_op jit(solution)/shard_map/mul | solution.py:908
  26.4 5.9 %all-to-all-done.1 = f32[16,1,4608]{2,1,0:T(1,128)} async-done(((f32[16,1,4608]{2,1,0:T(1,128)}), f32[16,1,4608]{2,1,0:T(1,128)}, u32[]{:S(2)}, u32[]{:S(2)}) %all-to-all-start.1) | async-done | bytes 294944 | tf_op jit(solution)/shard_map/all_to_all | solution.py:913
  44.4 13.1 %shard_map.256 = (bf16[3,2,2,1024,512]{4,3,2,1,0:T(8,128)(2,1)}, bf16[384,1024]{1,0:T(8,128)(2,1)S(1)}, f32[3,2,1,1024]{3,2,1,0:T(1,128)S(1)}, f32[512,768]{1,0:T(8,128)S(1)}, bf16[512,768]{1,0:T(8,128)(2,1)S(1)}) custom-call(s32[2]{0:T(128)S(1)} %add_clamp_fusion.refs_0_, bf16[3,1024,384]{2,1,0:T(8,128)(2,1)S(1)} %shard_map.255.refs_1_.refs_2_.refs_3_.refs_0_, ...), custom_call_target="tpu_custom_call" | custom-call | tf_op jit(solution)/shard_map/pallas_call | solution.py:40
  68.5 9.5 %shard_map.259 = (bf16[768,768]{1,0:T(8,128)(2,1)}, bf16[768,768]{1,0:T(8,128)(2,1)S(1)}, bf16[1024,768]{1,0:T(8,128)(2,1)S(1)}, bf16[1024,768]{1,0:T(8,128)(2,1)S(1)}, f32[1,768]{1,0:T(1,128)S(1)}) custom-call(s32[1]{0:T(128)} %bitcast.7.refs_0_, bf16[512,768]{1,0:T(8,128)(2,1)} %get-tuple-element.91.refs_1_, ...), custom_call_target="tpu_custom_call" | custom-call | tf_op jit(solution)/shard_map/pallas_call | solution.py:40
  79.1 10.0 %shard_map.260 = (bf16[768,768]{1,0:T(8,128)(2,1)}, bf16[768,768]{1,0:T(8,128)(2,1)S(1)}, bf16[1024,768]{1,0:T(8,128)(2,1)S(1)}, bf16[1024,768]{1,0:T(8,128)(2,1)S(1)}, f32[1,768]{1,0:T(1,128)S(1)}) custom-call(s32[1]{0:T(128)} %bitcast.7.refs_0_, bf16[512,768]{1,0:T(8,128)(2,1)} %get-tuple-element.91.refs_1_, ...), custom_call_target="tpu_custom_call" | custom-call | tf_op jit(solution)/shard_map/pallas_call | solution.py:40
  92.0 5.8 %collective-permute-start.7 = (bf16[768,768]{1,0:T(8,128)(2,1)}, bf16[768,768]{1,0:T(8,128)(2,1)}, u32[]{:S(2)}, u32[]{:S(2)}) collective-permute-start(bf16[768,768]{1,0:T(8,128)(2,1)} %get-tuple-element.95.refs_8_), channel_id=1, source_target_pairs={{0,2},{1,5},{2,0},{3,7},{4,6},{5,1},{6,4},{7,3},{8,10},{9,13},{10,... | collective-permute-start | bytes 3538952 | tf_op jit(solution)/shard_map/mlp_first/ppermute | solution.py:559
  101.6 3.1 %shard_map.263 = (f32[512,768]{1,0:T(8,128)S(1)}, bf16[512,768]{1,0:T(8,128)(2,1)}, f32[8,768]{1,0:T(8,128)S(1)}) custom-call(s32[2]{0:T(128)S(1)} %add_clamp_fusion.refs_0_, bf16[512,768]{1,0:T(8,128)(2,1)S(1)} %bitcast.59, bf16[512,768]{1,0:T(8,128)(2,1)S(1)} %bitcast.65, f32[512,768]{1,0:T(8,128)S(1)} %copy-done.32, ...), custom_call_target="tpu_custom_call" | custom-call | tf_op jit(solution)/shard_map/pallas_call | solution.py:40
  105.9 6.4 %collective-permute-done.7.refs_2_ = bf16[768,768]{1,0:T(8,128)(2,1)} collective-permute-done((bf16[768,768]{1,0:T(8,128)(2,1)}, bf16[768,768]{1,0:T(8,128)(2,1)}, u32[]{:S(2)}, u32[]{:S(2)}) %collective-permute-start.7) | collective-permute-done | bytes 1179680 | tf_op jit(solution)/shard_map/mlp_first/ppermute | solution.py:559
  113.6 2.8 mlp_first.6
  116.4 3.0 %shard_map.264 = (bf16[384,1024]{1,0:T(8,128)(2,1)S(1)}, bf16[768,384]{1,0:T(8,128)(2,1)S(1)}) custom-call(bf16[512,768]{1,0:T(8,128)(2,1)} %get-tuple-element.107.refs_3_.refs_0_, bf16[512,768]{1,0:T(8,128)(2,1)} %collective-permute-done.6.refs_1_, bf16[384,768]{1,0:T(8,128)(2,1)S(1)} %copy-done.37, bf16[384,1024]{1,0:T(8,128)(2,1)S(1)} %copy-done.22, ...), custom_call_target="tpu_custom_call" | custom-call | tf_op jit(solution)/shard_map/pallas_call | solution.py:40
  120.3 6.9 %shard_map.265 = (bf16[768,384]{1,0:T(8,128)(2,1)S(1)}, bf16[1024,384]{1,0:T(8,128)(2,1)S(1)}, f32[1,384]{1,0:T(1,128)S(1)}) custom-call(bf16[3,1024,384]{2,1,0:T(8,128)(2,1)S(1)} %shard_map.255.refs_1_.refs_2_.refs_3_.refs_0_, bf16[3,2,2,1024,512]{4,3,2,1,0:T(8,128)(2,1)} %get-tuple-element.103.refs_1_, bf16[384,1024]{1,0:T(8,128)(2,1)S(1)} %copy-done.22, ...), custom_call_target="tpu_custom_call" | custom-call | tf_op jit(solution)/shard_map/pallas_call | solution.py:40
  127.2 3.5 %collective-permute-done.9.refs_2_ = bf16[768,768]{1,0:T(8,128)(2,1)} collective-permute-done((bf16[768,768]{1,0:T(8,128)(2,1)}, bf16[768,768]{1,0:T(8,128)(2,1)}, u32[]{:S(2)}, u32[]{:S(2)}) %collective-permute-start.9) | collective-permute-done | bytes 1179680 | tf_op jit(solution)/shard_map/mlp_second/ppermute | solution.py:559
  130.7 2.7 mlp_second.6
  141.3 6.6 %shard_map.266 = (bf16[768,384]{1,0:T(8,128)(2,1)S(1)}, bf16[1024,384]{1,0:T(8,128)(2,1)S(1)}, f32[1,384]{1,0:T(1,128)S(1)}) custom-call(bf16[3,1024,384]{2,1,0:T(8,128)(2,1)S(1)} %shard_map.255.refs_1_.refs_2_.refs_3_.refs_0_, bf16[3,2,2,1024,512]{4,3,2,1,0:T(8,128)(2,1)} %get-tuple-element.103.refs_1_, bf16[384,1024]{1,0:T(8,128)(2,1)S(1)} %copy-done.23, ...), custom_call_target="tpu_custom_call" | custom-call | tf_op jit(solution)/shard_map/pallas_call | solution.py:40
  149.4 6.7 %shard_map.267 = (bf16[768,384]{1,0:T(8,128)(2,1)S(1)}, bf16[1024,384]{1,0:T(8,128)(2,1)S(1)}, f32[1,384]{1,0:T(1,128)S(1)}) custom-call(bf16[3,1024,384]{2,1,0:T(8,128)(2,1)S(1)} %shard_map.255.refs_1_.refs_2_.refs_3_.refs_0_, bf16[3,2,2,1024,512]{4,3,2,1,0:T(8,128)(2,1)} %get-tuple-element.103.refs_1_, bf16[384,1024]{1,0:T(8,128)(2,1)S(1)} %copy-done.23, ...), custom_call_target="tpu_custom_call" | custom-call | tf_op jit(solution)/shard_map/pallas_call | solution.py:40
  166.4 6.4 %collective-permute-done.15.refs_1_ = bf16[192,768]{1,0:T(8,128)(2,1)S(1)} collective-permute-done((bf16[192,768]{1,0:T(8,128)(2,1)S(1)}, bf16[192,768]{1,0:T(8,128)(2,1)S(1)}, u32[]{:S(2)}, u32[]{:S(2)}) %collective-permute-start.15) | collective-permute-done | bytes 294944 | tf_op jit(solution)/shard_map/mlp_second/ppermute | solution.py:559
  175.4 11.8 %collective-permute-done.14.refs_1_ = bf16[192,768]{1,0:T(8,128)(2,1)S(1)} collective-permute-done((bf16[192,768]{1,0:T(8,128)(2,1)S(1)}, bf16[192,768]{1,0:T(8,128)(2,1)S(1)}, u32[]{:S(2)}, u32[]{:S(2)}) %collective-permute-start.14) | collective-permute-done | bytes 294944 | tf_op jit(solution)/shard_map/mlp_first/ppermute | solution.py:559
  193.5 5.6 %collective-permute-done.18.refs_2_ = bf16[192,768]{1,0:T(8,128)(2,1)S(1)} collective-permute-done((bf16[192,768]{1,0:T(8,128)(2,1)S(1)}, bf16[192,768]{1,0:T(8,128)(2,1)S(1)}, u32[]{:S(2)}, u32[]{:S(2)}) %collective-permute-start.18) | collective-permute-done | bytes 294944 | tf_op jit(solution)/shard_map/mlp_first/ppermute | solution.py:559
  202.5 6.5 %collective-permute-done.23.refs_2_ = bf16[192,768]{1,0:T(8,128)(2,1)S(1)} collective-permute-done((bf16[192,768]{1,0:T(8,128)(2,1)S(1)}, bf16[192,768]{1,0:T(8,128)(2,1)S(1)}, u32[]{:S(2)}, u32[]{:S(2)}) %collective-permute-start.23) | collective-permute-done | bytes 294944 | tf_op jit(solution)/shard_map/mlp_second/ppermute | solution.py:559
  213.5 6.9 %collective-permute-done.21.refs_1_ = bf16[192,768]{1,0:T(8,128)(2,1)S(1)} collective-permute-done((bf16[192,768]{1,0:T(8,128)(2,1)S(1)}, bf16[192,768]{1,0:T(8,128)(2,1)S(1)}, u32[]{:S(2)}, u32[]{:S(2)}) %collective-permute-start.21) | collective-permute-done | bytes 294944 | tf_op jit(solution)/shard_map/projections/ppermute | solution.py:559
  220.7 8.8 %collective-permute-done.20.refs_1_ = bf16[32,768]{1,0:T(8,128)(2,1)S(1)} collective-permute-done((bf16[32,768]{1,0:T(8,128)(2,1)S(1)}, bf16[32,768]{1,0:T(8,128)(2,1)S(1)}, u32[]{:S(2)}, u32[]{:S(2)}) %collective-permute-start.20) | collective-permute-done | bytes 49184 | tf_op jit(solution)/shard_map/ppermute | solution.py:559
  230.7 4.3 %collective-permute-done.25.refs_1_ = bf16[192,768]{1,0:T(8,128)(2,1)S(1)} collective-permute-done((bf16[192,768]{1,0:T(8,128)(2,1)S(1)}, bf16[192,768]{1,0:T(8,128)(2,1)S(1)}, u32[]{:S(2)}, u32[]{:S(2)}) %collective-permute-start.25) | collective-permute-done | bytes 294944 | tf_op jit(solution)/shard_map/projections/ppermute | solution.py:559
  235.9 5.1 %collective-permute-done.24.refs_1_ = bf16[64,768]{1,0:T(8,128)(2,1)S(1)} collective-permute-done((bf16[64,768]{1,0:T(8,128)(2,1)S(1)}, bf16[64,768]{1,0:T(8,128)(2,1)S(1)}, u32[]{:S(2)}, u32[]{:S(2)}) %collective-permute-start.24) | collective-permute-done | bytes 98336 | tf_op jit(solution)/shard_map/ppermute | solution.py:559
  248.5 3.9 %collective-permute-done.27.refs_1_ = bf16[128,768]{1,0:T(8,128)(2,1)S(1)} collective-permute-done((bf16[128,768]{1,0:T(8,128)(2,1)S(1)}, bf16[128,768]{1,0:T(8,128)(2,1)S(1)}, u32[]{:S(2)}, u32[]{:S(2)}) %collective-permute-start.27) | collective-permute-done | bytes 196640 | tf_op jit(solution)/shard_map/ppermute | solution.py:559
  254.6 3.8 %shard_map.278 = (f32[1536,768]{1,0:T(8,128)}, f32[768,1536]{1,0:T(8,128)}) custom-call(s32[1]{0:T(128)} %bitcast.7.refs_0_, bf16[768,768]{1,0:T(8,128)(2,1)S(1)} %mlp_second.11.refs_2_.refs_1_, bf16[768,768]{1,0:T(8,128)(2,1)} %collective-permute-done.32.refs_2_, ...), custom_call_target="tpu_custom_call", output_to_operand_aliasing={{0}: (3, {}), {1}: (4, {})} | custom-call | tf_op jit(solution)/shard_map/pallas_call | solution.py:40
  262.1 10.4 %collective-permute-done.30.refs_1_ = bf16[256,768]{1,0:T(8,128)(2,1)} collective-permute-done((bf16[256,768]{1,0:T(8,128)(2,1)S(1)}, bf16[256,768]{1,0:T(8,128)(2,1)}, u32[]{:S(2)}, u32[]{:S(2)}) %collective-permute-start.30) | collective-permute-done | bytes 393248 | tf_op jit(solution)/shard_map/ppermute | solution.py:559
  275.1 4.5 %all-to-all-start.2 = ((f32[16,1,48]{2,1,0:T(1,128)}), f32[16,1,48]{2,1,0:T(1,128)S(1)}, u32[]{:S(2)}, u32[]{:S(2)}) async-start(f32[16,1,48]{2,1,0:T(1,128)} %bitcast.15), calls=%async_computation.2 | async-start | bytes 16384 | tf_op jit(solution)/shard_map/all_to_all | solution.py:1027
  283.7 3.1 %all-to-all-done.2 = f32[16,1,48]{2,1,0:T(1,128)S(1)} async-done(((f32[16,1,48]{2,1,0:T(1,128)}), f32[16,1,48]{2,1,0:T(1,128)S(1)}, u32[]{:S(2)}, u32[]{:S(2)}) %all-to-all-start.2) | async-done | bytes 3104 | tf_op jit(solution)/shard_map/all_to_all | solution.py:1027
  288.6 3.8 %shard_map.280 = (f32[3,768,384]{2,1,0:T(8,128)}, f32[384,768]{1,0:T(8,128)}) custom-call(s32[1]{0:T(128)} %bitcast.7.refs_0_, bf16[768,768]{1,0:T(8,128)(2,1)S(1)} %projections.11.refs_2_.refs_1_, bf16[768,768]{1,0:T(8,128)(2,1)} %collective-permute-done.33.refs_2_, bf16[512,768]{1,0:T(8,128)(2,1)S(1)} %shard_map.279.refs_3_), custom_call_target="tpu_custom_call" | custom-call | tf_op jit(solution)/shard_map/pallas_call | solution.py:40
  (273 shorter events, 99.4 us)
Async XLA Ops:
  2.1 15.5 %all-to-all-start = ((bf16[1,16,48]{2,0,1:T(2,128)(2,1)}), bf16[1,16,48]{2,0,1:T(2,128)(2,1)S(1)}, u32[]{:S(2)}, u32[]{:S(2)}) async-start(bf16[1,16,48]{2,0,1:T(2,128)(2,1)} %all_to_all.38), calls=%async_computation | async-start | bytes 16384 | tf_op jit(solution)/shard_map/all_to_all | solution.py:911
  18.8 13.5 %all-to-all-start.1 = ((f32[16,1,4608]{2,1,0:T(1,128)}), f32[16,1,4608]{2,1,0:T(1,128)}, u32[]{:S(2)}, u32[]{:S(2)}) async-start(f32[16,1,4608]{2,1,0:T(1,128)} %copy.38), calls=%async_computation.1 | async-start | bytes 589824 | tf_op jit(solution)/shard_map/all_to_all | solution.py:913
  91.8 9.8 %collective-permute-start.5 = (bf16[512,768]{1,0:T(8,128)(2,1)S(1)}, bf16[512,768]{1,0:T(8,128)(2,1)S(1)}, u32[]{:S(2)}, u32[]{:S(2)}) collective-permute-start(bf16[512,768]{1,0:T(8,128)(2,1)S(1)} %get-tuple-element.100.refs_3_), channel_id=1, source_target_pairs={{0,1},{1,0},{2,3},{3,2},{4,5},{5,4},{6,7},{7,6},{8,9},{9,8},{10,11... | collective-permute-start | bytes 2359304 | tf_op jit(solution)/shard_map/ppermute | solution.py:550
  92.0 20.3 %collective-permute-start.7 = (bf16[768,768]{1,0:T(8,128)(2,1)}, bf16[768,768]{1,0:T(8,128)(2,1)}, u32[]{:S(2)}, u32[]{:S(2)}) collective-permute-start(bf16[768,768]{1,0:T(8,128)(2,1)} %get-tuple-element.95.refs_8_), channel_id=1, source_target_pairs={{0,2},{1,5},{2,0},{3,7},{4,6},{5,1},{6,4},{7,3},{8,10},{9,13},{10,... | collective-permute-start | bytes 3538952 | tf_op jit(solution)/shard_map/mlp_first/ppermute | solution.py:559
  97.8 32.9 %collective-permute-start.9 = (bf16[768,768]{1,0:T(8,128)(2,1)}, bf16[768,768]{1,0:T(8,128)(2,1)}, u32[]{:S(2)}, u32[]{:S(2)}) collective-permute-start(bf16[768,768]{1,0:T(8,128)(2,1)} %get-tuple-element.99.refs_3_), channel_id=1, source_target_pairs={{0,2},{1,5},{2,0},{3,7},{4,6},{5,1},{6,4},{7,3},{8,10},{9,13},{10,... | collective-permute-start | bytes 3538952 | tf_op jit(solution)/shard_map/mlp_second/ppermute | solution.py:559
  105.9 10.5 %collective-permute-start.6 = (bf16[512,768]{1,0:T(8,128)(2,1)}, bf16[512,768]{1,0:T(8,128)(2,1)}, u32[]{:S(2)}, u32[]{:S(2)}) collective-permute-start(bf16[512,768]{1,0:T(8,128)(2,1)} %get-tuple-element.107.refs_3_.refs_0_), channel_id=1, source_target_pairs={{0,1},{1,0},{2,3},{3,2},{4,5},{5,4},{6,7},{7,6},{8,9},{9,8},{10,11... | collective-permute-start | bytes 2359304 | tf_op jit(solution)/shard_map/ppermute | solution.py:550
  116.4 18.7 %collective-permute-start.8 = (bf16[384,768]{1,0:T(8,128)(2,1)}, bf16[384,768]{1,0:T(8,128)(2,1)}, u32[]{:S(2)}, u32[]{:S(2)}) collective-permute-start(bf16[384,768]{1,0:T(8,128)(2,1)} %get-tuple-element.109.refs_4_), channel_id=1, source_target_pairs={{0,4},{1,3},{2,6},{3,1},{4,0},{5,7},{6,2},{7,5},{8,12},{9,11},{10,... | collective-permute-start | bytes 1769480 | tf_op jit(solution)/shard_map/mlp_first/ppermute | solution.py:559
  135.1 12.9 %collective-permute-start.11 = (bf16[384,768]{1,0:T(8,128)(2,1)}, bf16[384,768]{1,0:T(8,128)(2,1)}, u32[]{:S(2)}, u32[]{:S(2)}) collective-permute-start(bf16[384,768]{1,0:T(8,128)(2,1)} %get-tuple-element.115.refs_3_), channel_id=1, source_target_pairs={{0,4},{1,3},{2,6},{3,1},{4,0},{5,7},{6,2},{7,5},{8,12},{9,11},{10,... | collective-permute-start | bytes 1769480 | tf_op jit(solution)/shard_map/mlp_second/ppermute | solution.py:559
  137.8 11.5 %collective-permute-start.10 = (bf16[192,768]{1,0:T(8,128)(2,1)S(1)}, bf16[192,768]{1,0:T(8,128)(2,1)S(1)}, u32[]{:S(2)}, u32[]{:S(2)}) collective-permute-start(bf16[192,768]{1,0:T(8,128)(2,1)S(1)} %get-tuple-element.116.refs_9_), channel_id=1, source_target_pairs={{0,8},{1,9},{2,10},{3,11},{4,12},{5,13},{6,14},{7,15},{8,0},{9,1},... | collective-permute-start | bytes 884744 | tf_op jit(solution)/shard_map/mlp_first/ppermute | solution.py:559
  156.6 30.8 %collective-permute-start.13 = (bf16[768,768]{1,0:T(8,128)(2,1)S(1)}, bf16[768,768]{1,0:T(8,128)(2,1)S(1)}, u32[]{:S(2)}, u32[]{:S(2)}) collective-permute-start(bf16[768,768]{1,0:T(8,128)(2,1)S(1)} %get-tuple-element.125.refs_4_), channel_id=1, source_target_pairs={{0,2},{1,5},{2,0},{3,7},{4,6},{5,1},{6,4},{7,3},{8,10},{9,13},{10,... | collective-permute-start | bytes 3538952 | tf_op jit(solution)/shard_map/projections/ppermute | solution.py:559
  159.0 5.2 %collective-permute-start.4 = (bf16[512,768]{1,0:T(8,128)(2,1)S(1)}, bf16[512,768]{1,0:T(8,128)(2,1)S(1)}, u32[]{:S(2)}, u32[]{:S(2)}) collective-permute-start(bf16[512,768]{1,0:T(8,128)(2,1)S(1)} %copy-done.47), channel_id=1, source_target_pairs={{0,1},{1,0},{2,3},{3,2},{4,5},{5,4},{6,7},{7,6},{8,9},{9,8},{10,11... | collective-permute-start | bytes 2359304 | tf_op jit(solution)/shard_map/ppermute | solution.py:550
  161.7 28.5 %collective-permute-start.12 = (bf16[512,768]{1,0:T(8,128)(2,1)S(1)}, bf16[512,768]{1,0:T(8,128)(2,1)S(1)}, u32[]{:S(2)}, u32[]{:S(2)}) collective-permute-start(bf16[512,768]{1,0:T(8,128)(2,1)S(1)} %get-tuple-element.126.refs_7_), channel_id=1, source_target_pairs={{0,1},{1,0},{2,3},{3,2},{4,5},{5,4},{6,7},{7,6},{8,9},{9,8},{10,11... | collective-permute-start | bytes 2359304 | tf_op jit(solution)/shard_map/ppermute | solution.py:550
  162.2 10.5 %collective-permute-start.15 = (bf16[192,768]{1,0:T(8,128)(2,1)S(1)}, bf16[192,768]{1,0:T(8,128)(2,1)S(1)}, u32[]{:S(2)}, u32[]{:S(2)}) collective-permute-start(bf16[192,768]{1,0:T(8,128)(2,1)S(1)} %get-tuple-element.121.refs_2_), channel_id=1, source_target_pairs={{0,8},{1,9},{2,10},{3,11},{4,12},{5,13},{6,14},{7,15},{8,0},{9,1},... | collective-permute-start | bytes 884744 | tf_op jit(solution)/shard_map/mlp_second/ppermute | solution.py:559
  164.2 23.0 %collective-permute-start.14 = (bf16[192,768]{1,0:T(8,128)(2,1)S(1)}, bf16[192,768]{1,0:T(8,128)(2,1)S(1)}, u32[]{:S(2)}, u32[]{:S(2)}) collective-permute-start(bf16[192,768]{1,0:T(8,128)(2,1)S(1)} %mlp_first.8.refs_9_.refs_0_), channel_id=1, source_target_pairs={{0,16},{1,17},{2,18},{3,19},{4,20},{5,21},{6,22},{7,23},{8,24},{9,... | collective-permute-start | bytes 884744 | tf_op jit(solution)/shard_map/mlp_first/ppermute | solution.py:559
  174.0 19.5 %collective-permute-start.19 = (bf16[192,768]{1,0:T(8,128)(2,1)S(1)}, bf16[192,768]{1,0:T(8,128)(2,1)S(1)}, u32[]{:S(2)}, u32[]{:S(2)}) collective-permute-start(bf16[192,768]{1,0:T(8,128)(2,1)S(1)} %mlp_second.8.refs_2_.refs_0_), channel_id=1, source_target_pairs={{0,16},{1,17},{2,18},{3,19},{4,20},{5,21},{6,22},{7,23},{8,24},{9,... | collective-permute-start | bytes 884744 | tf_op jit(solution)/shard_map/mlp_second/ppermute | solution.py:559
  187.3 11.8 %collective-permute-start.18 = (bf16[192,768]{1,0:T(8,128)(2,1)S(1)}, bf16[192,768]{1,0:T(8,128)(2,1)S(1)}, u32[]{:S(2)}, u32[]{:S(2)}) collective-permute-start(bf16[192,768]{1,0:T(8,128)(2,1)S(1)} %mlp_first.9.refs_3_.refs_1_), channel_id=1, source_target_pairs={{0,8},{1,9},{2,10},{3,11},{4,12},{5,13},{6,14},{7,15},{8,0},{9,1},... | collective-permute-start | bytes 884744 | tf_op jit(solution)/shard_map/mlp_first/ppermute | solution.py:559
  188.1 13.2 %collective-permute-start.17 = (bf16[384,768]{1,0:T(8,128)(2,1)S(1)}, bf16[384,768]{1,0:T(8,128)(2,1)S(1)}, u32[]{:S(2)}, u32[]{:S(2)}) collective-permute-start(bf16[384,768]{1,0:T(8,128)(2,1)S(1)} %get-tuple-element.132.refs_5_), channel_id=1, source_target_pairs={{0,4},{1,3},{2,6},{3,1},{4,0},{5,7},{6,2},{7,5},{8,12},{9,11},{10,... | collective-permute-start | bytes 1769480 | tf_op jit(solution)/shard_map/projections/ppermute | solution.py:559
  199.2 11.8 %collective-permute-start.22 = (bf16[384,768]{1,0:T(8,128)(2,1)S(1)}, bf16[384,768]{1,0:T(8,128)(2,1)S(1)}, u32[]{:S(2)}, u32[]{:S(2)}) collective-permute-start(bf16[384,768]{1,0:T(8,128)(2,1)S(1)} %mlp_first.10.refs_3_.refs_1_), channel_id=1, source_target_pairs={{0,4},{1,3},{2,6},{3,1},{4,0},{5,7},{6,2},{7,5},{8,12},{9,11},{10,... | collective-permute-start | bytes 1769480 | tf_op jit(solution)/shard_map/mlp_first/ppermute | solution.py:559
  201.3 7.7 %collective-permute-start.23 = (bf16[192,768]{1,0:T(8,128)(2,1)S(1)}, bf16[192,768]{1,0:T(8,128)(2,1)S(1)}, u32[]{:S(2)}, u32[]{:S(2)}) collective-permute-start(bf16[192,768]{1,0:T(8,128)(2,1)S(1)} %mlp_second.9.refs_3_.refs_1_), channel_id=1, source_target_pairs={{0,8},{1,9},{2,10},{3,11},{4,12},{5,13},{6,14},{7,15},{8,0},{9,1},... | collective-permute-start | bytes 884744 | tf_op jit(solution)/shard_map/mlp_second/ppermute | solution.py:559
  209.0 20.6 %collective-permute-start.26 = (bf16[384,768]{1,0:T(8,128)(2,1)S(1)}, bf16[384,768]{1,0:T(8,128)(2,1)S(1)}, u32[]{:S(2)}, u32[]{:S(2)}) collective-permute-start(bf16[384,768]{1,0:T(8,128)(2,1)S(1)} %mlp_second.10.refs_3_.refs_1_), channel_id=1, source_target_pairs={{0,4},{1,3},{2,6},{3,1},{4,0},{5,7},{6,2},{7,5},{8,12},{9,11},{10,... | collective-permute-start | bytes 1769480 | tf_op jit(solution)/shard_map/mlp_second/ppermute | solution.py:559
  211.1 29.9 %collective-permute-start.29 = (bf16[768,768]{1,0:T(8,128)(2,1)S(1)}, bf16[768,768]{1,0:T(8,128)(2,1)S(1)}, u32[]{:S(2)}, u32[]{:S(2)}) collective-permute-start(bf16[768,768]{1,0:T(8,128)(2,1)S(1)} %mlp_first.11.refs_2_.refs_1_), channel_id=1, source_target_pairs={{0,2},{1,5},{2,0},{3,7},{4,6},{5,1},{6,4},{7,3},{8,10},{9,13},{10,... | collective-permute-start | bytes 3538952 | tf_op jit(solution)/shard_map/mlp_first/ppermute | solution.py:559
  212.2 8.2 %collective-permute-start.21 = (bf16[192,768]{1,0:T(8,128)(2,1)S(1)}, bf16[192,768]{1,0:T(8,128)(2,1)S(1)}, u32[]{:S(2)}, u32[]{:S(2)}) collective-permute-start(bf16[192,768]{1,0:T(8,128)(2,1)S(1)} %get-tuple-element.144.refs_7_), channel_id=1, source_target_pairs={{0,8},{1,9},{2,10},{3,11},{4,12},{5,13},{6,14},{7,15},{8,0},{9,1},... | collective-permute-start | bytes 884744 | tf_op jit(solution)/shard_map/projections/ppermute | solution.py:559
  212.5 17.1 %collective-permute-start.20 = (bf16[32,768]{1,0:T(8,128)(2,1)S(1)}, bf16[32,768]{1,0:T(8,128)(2,1)S(1)}, u32[]{:S(2)}, u32[]{:S(2)}) collective-permute-start(bf16[32,768]{1,0:T(8,128)(2,1)S(1)} %shard_map.273.refs_3_.refs_0_), channel_id=1, source_target_pairs={{0,2},{1,3},{2,0},{3,1},{4,6},{5,7},{6,4},{7,5},{8,10},{9,11},{10,... | collective-permute-start | bytes 147464 | tf_op jit(solution)/shard_map/ppermute | solution.py:559
  220.5 14.5 %collective-permute-start.25 = (bf16[192,768]{1,0:T(8,128)(2,1)S(1)}, bf16[192,768]{1,0:T(8,128)(2,1)S(1)}, u32[]{:S(2)}, u32[]{:S(2)}) collective-permute-start(bf16[192,768]{1,0:T(8,128)(2,1)S(1)} %projections.8.refs_2_.refs_0_), channel_id=1, source_target_pairs={{0,16},{1,17},{2,18},{3,19},{4,20},{5,21},{6,22},{7,23},{8,24},{9,... | collective-permute-start | bytes 884744 | tf_op jit(solution)/shard_map/projections/ppermute | solution.py:559
  229.7 24.9 %collective-permute-start.32 = (bf16[768,768]{1,0:T(8,128)(2,1)S(1)}, bf16[768,768]{1,0:T(8,128)(2,1)}, u32[]{:S(2)}, u32[]{:S(2)}) collective-permute-start(bf16[768,768]{1,0:T(8,128)(2,1)S(1)} %mlp_second.11.refs_2_.refs_1_), channel_id=1, source_target_pairs={{0,2},{1,5},{2,0},{3,7},{4,6},{5,1},{6,4},{7,3},{8,10},{9,13},{10,... | collective-permute-start | bytes 3538952 | tf_op jit(solution)/shard_map/mlp_second/ppermute | solution.py:559
  235.1 8.6 %collective-permute-start.28 = (bf16[192,768]{1,0:T(8,128)(2,1)S(1)}, bf16[192,768]{1,0:T(8,128)(2,1)S(1)}, u32[]{:S(2)}, u32[]{:S(2)}) collective-permute-start(bf16[192,768]{1,0:T(8,128)(2,1)S(1)} %projections.9.refs_2_.refs_1_), channel_id=1, source_target_pairs={{0,8},{1,9},{2,10},{3,11},{4,12},{5,13},{6,14},{7,15},{8,0},{9,1},... | collective-permute-start | bytes 884744 | tf_op jit(solution)/shard_map/projections/ppermute | solution.py:559
  235.2 5.8 %collective-permute-start.24 = (bf16[64,768]{1,0:T(8,128)(2,1)S(1)}, bf16[64,768]{1,0:T(8,128)(2,1)S(1)}, u32[]{:S(2)}, u32[]{:S(2)}) collective-permute-start(bf16[64,768]{1,0:T(8,128)(2,1)S(1)} %shard_map.274.refs_3_.refs_0_), channel_id=1, source_target_pairs={{0,4},{1,5},{2,6},{3,7},{4,0},{5,1},{6,2},{7,3},{8,12},{9,13},{10,... | collective-permute-start | bytes 294920 | tf_op jit(solution)/shard_map/ppermute | solution.py:559
  246.1 12.2 %collective-permute-start.31 = (bf16[384,768]{1,0:T(8,128)(2,1)S(1)}, bf16[384,768]{1,0:T(8,128)(2,1)S(1)}, u32[]{:S(2)}, u32[]{:S(2)}) collective-permute-start(bf16[384,768]{1,0:T(8,128)(2,1)S(1)} %projections.10.refs_2_.refs_1_), channel_id=1, source_target_pairs={{0,4},{1,3},{2,6},{3,1},{4,0},{5,7},{6,2},{7,5},{8,12},{9,11},{10,... | collective-permute-start | bytes 1769480 | tf_op jit(solution)/shard_map/projections/ppermute | solution.py:559
  246.7 5.7 %collective-permute-start.27 = (bf16[128,768]{1,0:T(8,128)(2,1)S(1)}, bf16[128,768]{1,0:T(8,128)(2,1)S(1)}, u32[]{:S(2)}, u32[]{:S(2)}) collective-permute-start(bf16[128,768]{1,0:T(8,128)(2,1)S(1)} %shard_map.275.refs_3_.refs_0_), channel_id=1, source_target_pairs={{0,8},{1,9},{2,10},{3,11},{4,12},{5,13},{6,14},{7,15},{8,0},{9,1},... | collective-permute-start | bytes 589832 | tf_op jit(solution)/shard_map/ppermute | solution.py:559
  252.4 20.1 %collective-permute-start.30 = (bf16[256,768]{1,0:T(8,128)(2,1)S(1)}, bf16[256,768]{1,0:T(8,128)(2,1)}, u32[]{:S(2)}, u32[]{:S(2)}) collective-permute-start(bf16[256,768]{1,0:T(8,128)(2,1)S(1)} %shard_map.277.refs_5_.refs_0_), channel_id=1, source_target_pairs={{0,16},{1,17},{2,18},{3,19},{4,20},{5,21},{6,22},{7,23},{8,24},{9,... | collective-permute-start | bytes 1179656 | tf_op jit(solution)/shard_map/ppermute | solution.py:559
  260.8 27.9 %collective-permute-start.33 = (bf16[768,768]{1,0:T(8,128)(2,1)S(1)}, bf16[768,768]{1,0:T(8,128)(2,1)}, u32[]{:S(2)}, u32[]{:S(2)}) collective-permute-start(bf16[768,768]{1,0:T(8,128)(2,1)S(1)} %projections.11.refs_2_.refs_1_), channel_id=1, source_target_pairs={{0,2},{1,5},{2,0},{3,7},{4,6},{5,1},{6,4},{7,3},{8,10},{9,13},{10,... | collective-permute-start | bytes 3538952 | tf_op jit(solution)/shard_map/projections/ppermute | solution.py:559
  275.1 11.7 %all-to-all-start.2 = ((f32[16,1,48]{2,1,0:T(1,128)}), f32[16,1,48]{2,1,0:T(1,128)S(1)}, u32[]{:S(2)}, u32[]{:S(2)}) async-start(f32[16,1,48]{2,1,0:T(1,128)} %bitcast.15), calls=%async_computation.2 | async-start | bytes 16384 | tf_op jit(solution)/shard_map/all_to_all | solution.py:1027
  (69 other events, 307.3 us)
where the time goes:
time: 293 us
  Pallas kernels  98.9 us (34%)
  waiting for transfers between devices  97.2 us (33%)
  starting transfers between devices  46.1 us (16%)
  local copies, waits for them, and re-layouts  37.4 us (13%)
  other arithmetic  8.67 us (3%)
    pallas_call x45, Pallas kernels, call(): pl.pallas_call(wrapped, grid=grid, in_specs=list(in_specs) + [pl.BlockSpe...  98.9 us
    ppermute x25, waiting for transfers between devices, bit_swap(): return lax.ppermute(value, ('dp', 'tensor'), pairs)  79.9 us
    unnamed x131, local copies, waits for them, and re-layouts  30.8 us
    ppermute x25, starting transfers between devices, bit_swap(): return lax.ppermute(value, ('dp', 'tensor'), pairs)  27.7 us
    all_to_all x1, starting transfers between devices, shards(): lax.all_to_all(temb, 'dp', split_axis=1, concat_axis=0, tiled=True)  8.31 us
    all_to_all x1, waiting for transfers between devices, shards(): lax.all_to_all(mod_terms, 'dp', split_axis=0, concat_axis=0, tiled=True)  5.94 us
  transfers between devices with their start and end apart: 37, of which 19 were waited for; matrix products, arithmetic and copies ran while one was open for 5% of the time, Pallas kernels for 17%

commit v1 on v0

v1 whole, which is shorter than its diff:
```python
from functools import partial
from math import log, pi, sqrt

import jax
import jax.numpy as jnp
from jax import lax
from jax.experimental import pallas as pl
from jax.experimental.pallas import tpu as pltpu
from jax.sharding import PartitionSpec as P

HEAD_DIM = 64
PAIR = 2 * HEAD_DIM
F32 = jnp.float32
BF16 = jnp.bfloat16
NN = ((1,), (0,))
NT = ((1,), (1,))
TN = ((0,), (0,))
SAFE = 90.0
LONG = 10**9
ORDER = (
    "mlp_first", "turn", "back", "mlp_second", "mlp_first", "d_attn_in", "mlp_second", "mlp_first",
    "finish", "end", "share", "mlp_second", "projections", "mlp_first", "projections", "begin",
    "mlp_first", "mlp_second", "projections", "small", "mlp_first", "projections", "small",
    "mlp_second", "unpack_first", "projections", "mlp_second", "small", "small", "projections",
    "unpack_second",
)
LN2 = log(2.0)
MIB = 1024 * 1024
VM = pl.BlockSpec(memory_space=pltpu.VMEM)
SM = pl.BlockSpec(memory_space=pltpu.SMEM)
HB = pl.BlockSpec(memory_space=pltpu.HBM)


def dot(left, right, dims=NN):
    return lax.dot_general(left, right, (dims, ((), ())), preferred_element_type=F32)


class Late:
    def __init__(self, *parts):
        self.parts = parts or ((),)


class Queue:
    def __init__(self, copies, ahead):
        self.copies = copies
        self.started = 0
        self.here = set()
        self.start(ahead)

    def start(self, count):
        for copy in self.copies[self.started : self.started + count]:
            copy.start()
        self.started += count

    def need(self, n):
        if n not in self.here:
            self.start(max(0, n + 1 - self.started))
            self.here.add(n)
            self.copies[n].wait()
            self.start(1)


class LateRef:
    def __init__(self, queue, places, refs):
        self.queue = queue
        self.places = places
        self.refs = refs

    def get(self, n=0):
        self.queue.need(self.places[n])
        return self.refs[n]


def call(body, grid, in_specs, out_specs, out_shape, args, scratch=(), line=None, room=12, aliases=None, ahead=3, rank=None, cost=None):
    count = len(in_specs)
    single = not isinstance(out_shape, list)
    out_specs = [out_specs] if single else list(out_specs)
    out_shape = [out_shape] if single else list(out_shape)
    outs = len(out_shape)
    late = [n for n, spec in enumerate(in_specs) if isinstance(spec, Late)]
    pieces = [(n, part) for n in late for part in in_specs[n].parts]
    if rank is not None:
        pieces.sort(key=lambda piece: rank(piece[0], in_specs[piece[0]].parts.index(piece[1])))
    buffers = [
        pltpu.VMEM(jax.eval_shape(lambda x, part=part: x[part], args[n]).shape, args[n].dtype)
        for n, part in pieces
    ]
    args = [far_core(arg) if n in late else arg for n, arg in enumerate(args)]
    in_specs = [HB if n in late else spec for n, spec in enumerate(in_specs)]
    if pieces:
        buffers.append(pltpu.SemaphoreType.DMA((len(pieces),)))
    extra = 0
    if line is not None:
        extra = 1
        cost = LONG if cost is None else cost
        in_specs.append(pl.BlockSpec(memory_space=pl.ANY))
        args.append(line.turn)
        out_specs.append(VM)
        out_shape.append(shape_of((8, 128), F32))

    def wrapped(*refs):
        ins = list(refs[:count])
        rest = list(refs[count + extra : count + extra + outs])
        if extra:
            refs[count + extra + outs][...] = jnp.zeros((8, 128), F32)
        rest += refs[count + 2 * extra + outs :]
        if pieces:
            rest, held, sems = rest[: -len(buffers)], rest[-len(buffers) : -1], rest[-1]
            copies = []
            for i, (n, part) in enumerate(pieces):
                source = ins[n].at[part] if part else ins[n]
                copies.append(pltpu.make_async_copy(source, held[i], sems.at[i]))
            queue = Queue(copies, ahead)
            for n in late:
                mine = [i for i, (m, _) in enumerate(pieces) if m == n]
                ins[n] = LateRef(queue, mine, [held[i] for i in mine])
        body(*ins, *rest)
        if pieces:
            for i in range(len(pieces)):
                queue.need(i)

    result = pl.pallas_call(
        wrapped,
        grid=grid,
        in_specs=in_specs,
        out_specs=out_specs,
        out_shape=out_shape,
        scratch_shapes=list(scratch) + buffers,
        input_output_aliases=aliases or {},
        compiler_params=pltpu.CompilerParams(
            vmem_limit_bytes=room * MIB, dimension_semantics=("arbitrary",) * len(grid)
        ),
        cost_estimate=pl.CostEstimate(flops=cost or 0, bytes_accessed=0, transcendentals=0),
    )(*args)
    if extra:
        line.turn = result[-1]
        result = result[:-1]
    return result[0] if single else result


def whole(shape):
    return pl.BlockSpec(shape, lambda *_: (0,) * len(shape))


def shape_of(shape, kind):
    return pltpu.VMEM(shape, kind)


def far_core(value):
    return pltpu.with_memory_space_constraint(value, pltpu.HBM)


def norm_parts(field):
    centred = field - jnp.mean(field, axis=-1, keepdims=True)
    inverse = lax.rsqrt(jnp.mean(centred * centred, axis=-1, keepdims=True) + 1e-05)
    return (centred * inverse, inverse)


def norm_back(upstream, normed, inverse):
    return inverse * (
        upstream
        - jnp.mean(upstream, axis=-1, keepdims=True)
        - normed * jnp.mean(upstream * normed, axis=-1, keepdims=True)
    )


def gelu_parts(hidden):
    scale = sqrt(2.0 / pi)
    square = hidden * hidden
    bent = jnp.tanh(hidden * (scale + (scale * 0.044715) * square))
    upper = 0.5 + 0.5 * bent
    slope = upper + (hidden * (0.5 - 0.5 * bent * bent)) * (scale + (3 * 0.044715 * scale) * square)
    return (hidden * upper, slope)


def turn_lanes(field):
    lane = lax.broadcasted_iota(jnp.int32, field.shape, 1)
    up = pltpu.roll(field, PAIR - HEAD_DIM // 2, 1)
    down = pltpu.roll(field, HEAD_DIM // 2, 1)
    return jnp.where((lane & (HEAD_DIM - 1)) < HEAD_DIM // 2, up, down)


def zero_other(field, h, axis):
    place = lax.broadcasted_iota(jnp.int32, field.shape, axis)
    return jnp.where((place >= HEAD_DIM) == (h == 1), field, jnp.zeros_like(field))


def total(field):
    return jnp.sum(field, axis=0, keepdims=True)


def both(near, far):
    return jnp.concatenate([near[...], far[...]], axis=0)


def attend_call(counts, near, far, weight, bias, cosine, sine, out_weight):
    rows, width = near.shape
    keys = 2 * rows
    half = weight.shape[2]
    pairs = half // PAIR
    quarter = HEAD_DIM // 2

    def body(
        cnt, xn, xf, w, b, cos, sin, w_out, e_out, ot_out, inv_out, near_out, far_out, qkv_out, trig, qkv, o_all, sem
    ):
        j = pl.program_id(0)
        store = pltpu.make_async_copy(qkv, qkv_out, sem.at[0])

        @pl.when(j == 0)
        def _():
            for c in range(3):
                for i, x in enumerate((xn, xf)):
                    here = slice(i * rows, (i + 1) * rows)
                    y = dot(x[...], w[c]) + b[c]
                    for n in range(pairs):
                        u = y[:, n * PAIR : (n + 1) * PAIR]
                        if c < 2:
                            u = u * cos[here] + turn_lanes(u) * sin[here]
                        if c == 0:
                            u = u * (HEAD_DIM ** (-0.5) / LN2)
                        qkv[c, n, here] = u.astype(BF16)
            trig[:quarter] = cos[...].T[:quarter]
            trig[quarter:] = sin[...].T[quarter : 2 * quarter]
            store.start()

        q_in = qkv.at[0, j]
        k = qkv[1, j]
        v_t = qkv[2, j].T
        near_count, far_count = cnt[0], cnt[1]

        def run(masked, plain):
            for p in range(2):
                of = slice(p * rows, (p + 1) * rows)
                q_t = q_in[of].T
                for h in range(2):
                    hs = slice(h * HEAD_DIM, (h + 1) * HEAD_DIM)
                    s = dot(k, zero_other(q_t, h, 0))
                    if masked:
                        place = lax.broadcasted_iota(jnp.int32, (keys, rows), 0)
                        limit = jnp.where(place < rows, near_count, rows + far_count)
                        s = jnp.where(place < limit, s, -1e30)
                    if not plain:
                        s = s - jnp.max(s, axis=0, keepdims=True)
                    e = jnp.exp2(s)
                    inv = 1.0 / total(e)
                    e = e.astype(BF16)
                    e_out[0, h, p] = e
                    inv_out[0, h, :, of] = inv
                    ot_out[hs, of] = (dot(v_t[hs], e) * inv).astype(BF16)

        def norms(field):
            square = field.astype(F32) * field.astype(F32)
            return [
                jnp.max(jnp.sum(zero_other(square, h, 1), axis=1, keepdims=True)) for h in range(2)
            ]

        bound = 0.0
        for one, two in zip(norms(q_in[...]), norms(k)):
            bound = jnp.maximum(bound, one * two)
        plain = bound < SAFE * SAFE
        everything = near_count + far_count >= keys
        pl.when(plain & everything)(lambda: run(False, True))
        pl.when(plain & jnp.logical_not(everything))(lambda: run(True, True))
        pl.when(jnp.logical_not(plain))(lambda: run(True, False))
        o_all[j] = ot_out[...].T

        @pl.when(j == pairs - 1)
        def _():
            o = jnp.concatenate([o_all[i] for i in range(pairs)], axis=1)
            near_out[...] = dot(o[:rows], w_out[...])
            far_out[...] = dot(o[rows:], w_out[...]).astype(BF16)
            store.wait()

    return call(
        body,
        (pairs,),
        [
            SM,
            whole((rows, width)),
            whole((rows, width)),
            whole((3, width, half)),
            whole((3, 1, half)),
            whole((keys, PAIR)),
            whole((keys, PAIR)),
            whole((half, width)),
        ],
        [
            pl.BlockSpec((1, 2, 2, keys, rows), lambda j: (j, 0, 0, 0, 0)),
            pl.BlockSpec((PAIR, keys), lambda j: (j, 0)),
            pl.BlockSpec((1, 2, 1, keys), lambda j: (j, 0, 0, 0)),
            whole((rows, width)),
            whole((rows, width)),
            HB,
            whole((HEAD_DIM, keys)),
        ],
        [
            pltpu.HBM((pairs, 2, 2, keys, rows), BF16),
            pltpu.HBM((half, keys), BF16),
            shape_of((pairs, 2, 1, keys), F32),
            shape_of((rows, width), F32),
            shape_of((rows, width), BF16),
            pltpu.HBM((3, pairs, keys, PAIR), BF16),
            shape_of((HEAD_DIM, keys), F32),
        ],
        (counts, near, far, far_core(weight), bias, far_core(cosine), far_core(sine), far_core(out_weight)),
        [
            pltpu.VMEM((3, pairs, keys, PAIR), BF16),
            pltpu.VMEM((pairs, keys, PAIR), BF16),
            pltpu.SemaphoreType.DMA((1,)),
        ],
        room=36,
    )


def middle_call(tokens, near, far, vecs):
    rows, width = tokens.shape

    def body(tok, nr, fr, vec, branch_out, fed_out):
        branch = nr[...] + fr[...].astype(F32)
        branch_out[...] = branch
        normed, _ = norm_parts(tok[...].astype(F32) + vec[2:3] * branch)
        fed_out[...] = (normed * vec[3:4] + vec[4:5]).astype(BF16)

    return call(
        body,
        (),
        [VM] * 4,
        [VM] * 2,
        [pltpu.HBM((rows, width), F32), shape_of((rows, width), BF16)],
        (tokens, near, far, vecs),
    )


def mlp_call(first, units, bits, fed, far, g, g_far, up, down, bias, before, line=None):
    rows, width = fed.shape
    tile = 256

    def body(bit, fed_in, far_in, g_in, gf_in, up_in, down_in, b_in, *rest):
        old, rest = rest[: len(before)], rest[len(before) :]
        send, keep, sums = rest[:3]
        act_out, dh_out = rest[-2:]
        step = rows // 2

        def run(down_to, up_to):
            for n in range(units // tile):
                here = slice(n * tile, (n + 1) * tile)
                there = slice(first + n * tile, first + (n + 1) * tile)
                up_w, down_w = up_in[:, there], down_in[there]
                for i in range(4):
                    x, gr = ((fed_in, g_in), (far_in, gf_in))[i // 2]
                    of, to = [slice(k * step, (k + 1) * step) for k in (i % 2, i)]
                    active, slope = gelu_parts(dot(x[of], up_w) + b_in[:, there])
                    act_out[to, here] = active.astype(BF16)
                    dh_out[to, here] = (dot(gr[of], down_w, NT) * slope).astype(BF16)
                down_to[here, :] = dot(act_out[:, here], both(g_in, gf_in), TN).astype(BF16)
                up_to[:, here] = dot(both(fed_in, far_in), dh_out[:, here], TN).astype(BF16)
                sums[:, here] = total(dh_out[:, here].astype(F32))

        pl.when(bit[0] == 0)(lambda: run(keep, send))
        pl.when(bit[0] != 0)(lambda: run(send, keep))

        if before:
            for i, place in enumerate((3, 5)):
                for k in range(2):
                    of = slice(k * rows, (k + 1) * rows)
                    low, high = old[1 - i][of], (dh_out, act_out)[i][of]
                    if i == 0:
                        value = dot(low, up_in[:, :first], NT) + dot(high, up_in[:, first:], NT)
                    else:
                        value = dot(low, down_in[:first]) + dot(high, down_in[first:])
                    rest[place + k][...] = value.astype(rest[place + k].dtype)

    both_rows = (2 * rows, units)
    out_specs = [VM] * 3
    out_shape = [pltpu.HBM((width, units), BF16)] * 2 + [shape_of((1, units), F32)]
    scratch = []
    if before:
        out_specs += [VM] * 4
        out_shape += [shape_of((rows, width), F32), shape_of((rows, width), BF16)]
        out_shape += [pltpu.HBM((rows, width), F32), pltpu.HBM((rows, width), BF16)]
        scratch = [pltpu.VMEM(both_rows, BF16)] * 2
    else:
        out_specs += [VM] * 2
        out_shape += [shape_of(both_rows, BF16)] * 2
    return call(
        body,
        (),
        [SM] + [VM] * (7 + len(before)),
        out_specs,
        out_shape,
        (bits, fed, far, g, g_far, up, down, bias, *before),
        scratch,
        line=line,
        room=16,
        cost=0,
    )


def rotary_tables(start, rows):
    quarter = HEAD_DIM // 2
    lane = lax.iota(jnp.int32, PAIR)
    frequency = 10000.0 ** (-(lane & (quarter - 1)).astype(F32) / quarter)
    sign = jnp.where((lane & quarter) == 0, -1.0, 1.0)
    order = lax.iota(jnp.int32, rows)
    places = jnp.concatenate([start + order, (rows - start) + order]).astype(F32)
    angles = places[:, None] * frequency[None, :]
    return jnp.cos(angles), jnp.sin(angles) * sign[None, :]


def input_call(normed, vecs):
    rows, width = normed.shape

    def body(n, vec, out, kept):
        value = (n[...] * vec[0:1] + vec[1:2]).astype(BF16)
        out[...] = value
        kept[...] = value

    return call(
        body,
        (),
        [VM, VM],
        [VM, VM],
        [shape_of((rows, width), BF16), pltpu.HBM((rows, width), BF16)],
        (normed, vecs),
    )


def masked(cnt, field):
    place = lax.broadcasted_iota(jnp.int32, field.shape, 0)
    return jnp.where(place < cnt[0], field.astype(F32), 0.0)


def upstream_call(counts, cotangent, vecs):
    rows, width = cotangent.shape

    def body(cnt, cot, vec, g_out, sum_out):
        g = (masked(cnt, cot[...]) * vec[5:6]).astype(BF16)
        g_out[...] = g
        sum_out[...] = total(g.astype(F32))

    return call(
        body,
        (),
        [SM, VM, VM],
        [VM, VM],
        [shape_of((rows, width), BF16), shape_of((1, width), F32)],
        (counts, cotangent, vecs),
    )


def turn_call(counts, tokens, cotangent, branch, d_near, d_far, vecs, line=None):
    rows, width = tokens.shape

    def body(cnt, tok, cot, br, dn, df, vec, dm_out, g_out, sum_out):
        normed, inverse = norm_parts(tok[...].astype(F32) + vec[2:3] * br[...])
        d_in = dn[...] + df[...].astype(F32)
        d_middle = masked(cnt, cot[...]) + norm_back(d_in * vec[3:4], normed, inverse)
        g_out[...] = (d_middle * vec[2:3]).astype(BF16)
        dm_out[...] = d_middle
        sum_out[0:1] = total(d_middle * br[...])
        sum_out[1:2] = total(d_in)
        sum_out[2:3] = total(d_in * normed)
        sum_out[3:8] = jnp.zeros((5, width), F32)

    return call(
        body,
        (),
        [SM] + [VM] * 6,
        [VM] * 3,
        [pltpu.HBM((rows, width), F32), shape_of((rows, width), BF16), shape_of((8, width), F32)],
        (counts, tokens, cotangent, branch, d_near, d_far, vecs),
        line=line,
    )


def finish_call(counts, tokens, cotangent, branch, b_near, b_far, vecs, line=None):
    rows, width = tokens.shape

    def body(cnt, tok, cot, br, bn, bf, vec, y_out, sum_out):
        middle = tok[...].astype(F32) + vec[2:3] * br[...]
        mlp_branch = bn[...] + bf[...].astype(F32) + vec[6:7]
        y_out[...] = masked(cnt, middle + vec[5:6] * mlp_branch).astype(BF16)
        sum_out[0:1] = total(masked(cnt, cot[...]) * mlp_branch)
        sum_out[1:8] = jnp.zeros((7, width), F32)

    return call(
        body,
        (),
        [SM] + [VM] * 6,
        [VM] * 2,
        [pltpu.HBM((rows, width), BF16), shape_of((8, width), F32)],
        (counts, tokens, cotangent, branch, b_near, b_far, vecs),
        line=line,
    )


def attend_back_call(bits, g, g_far, weight, qkv, e, o_t, inv, trig, cosine, sine, near, far, line=None):
    _, pairs, keys, _ = qkv.shape
    rows, width = near.shape
    half = weight.shape[0]
    quarter = HEAD_DIM // 2
    size = 3 * PAIR

    def body(bit, g_in, gf_in, inv_in, turn, w_late, ot_late, qkv_late, e_late, xn, xf, cos, sin, *rest):
        send, keep, sums = rest[:3]
        d_alls, d_in = rest[3 : 3 + pairs], rest[-1]
        d_in[...] = dot(w_late.get()[...], both(g_in, gf_in), NT).astype(BF16)
        cos_t, sin_t = turn.at[:quarter], turn.at[quarter:]

        def put(block, fill):
            at = slice((block % 2) * size, (block % 2 + 1) * size)
            pl.when(bit[0] == block // 2)(lambda: fill(keep, at))
            pl.when(bit[0] != block // 2)(lambda: fill(send, at))

        def fill_pair(j, ref, at):
            ref[:, at] = dot(both(xn.get(), xf.get()), d_alls[j][...], TN).astype(BF16)

        def fill_out(ref, at):
            grad = dot(ot_late.get()[...], both(g_in, gf_in)).astype(BF16)
            ref[:half, at] = grad[:, :half]
            ref[half:, at] = grad[:, half:]

        for j in range(pairs):
            k_t = qkv_late.get(3 * j + 1)[...].T
            v = qkv_late.get(3 * j + 2)[...]
            d_k = d_v = 0.0
            d_q = []
            for p in range(2):
                of = slice(p * rows, (p + 1) * rows)
                scaled = []
                for h in range(2):
                    hs = slice(j * PAIR + h * HEAD_DIM, j * PAIR + (h + 1) * HEAD_DIM)
                    scaled.append((d_in[hs, of].astype(F32) * inv_in[j, h, :, of]).astype(BF16))
                d_t = jnp.concatenate(scaled, axis=0)
                d = d_t.T
                q = qkv_late.get(3 * j)[of]
                halves = []
                for h in range(2):
                    hs = slice(h * HEAD_DIM, (h + 1) * HEAD_DIM)
                    ot = ot_late.get()[j * PAIR + h * HEAD_DIM : j * PAIR + (h + 1) * HEAD_DIM, of]
                    delta = total(d_t[hs].astype(F32) * ot.astype(F32))
                    d_p = dot(v, zero_other(d_t, h, 0))
                    weight = e_late.get(4 * j + 2 * p + h)[...]
                    d_s = (weight.astype(F32) * (d_p - delta)).astype(BF16)
                    d_v = d_v + dot(weight, zero_other(d, h, 1))
                    d_k = d_k + dot(d_s, zero_other(q, h, 1))
                    t = dot(k_t[hs], d_s) * HEAD_DIM ** (-0.5)
                    one, two = t[:quarter], t[quarter:]
                    halves.append((one * cos_t[:, of] + two * sin_t[:, of]).astype(BF16))
                    halves.append((two * cos_t[:, of] - one * sin_t[:, of]).astype(BF16))
                d_q.append(jnp.concatenate(halves, axis=0).T)
            u = d_k * LN2
            d_k = (u * cos.get()[...] - turn_lanes(u) * sin.get()[...]).astype(BF16)
            every = jnp.concatenate([jnp.concatenate(d_q, axis=0), d_k, d_v.astype(BF16)], axis=1)
            d_alls[j][...] = every
            xn.get(), xf.get()
            put(j, partial(fill_pair, j))
            sums[j : j + 1] = total(every.astype(F32))
        put(pairs, fill_out)

    def rank(n, i):
        if n == 7:
            return (i // 3, 1, 0)
        if n == 8:
            return (i // 4, 2, i)
        return (0, 0, n) if n < 7 else (0, 3, n)

    return call(
        body,
        (),
        [SM, VM, VM, VM, VM, Late(), Late()]
        + [Late(*[(c, j) for j in range(pairs) for c in range(3)])]
        + [Late(*[(j, h, p) for j in range(pairs) for p in range(2) for h in range(2)])]
        + [Late()] * 4,
        [VM] * (3 + pairs),
        [shape_of((width, 2 * size), BF16)] * 2
        + [shape_of((pairs, size), F32)]
        + [shape_of((keys, size), BF16)] * pairs,
        (bits, g, g_far, inv, trig, weight, o_t, qkv, e, near, far, cosine, sine),
        [pltpu.VMEM((half, keys), BF16)],
        line=line,
        room=40,
        ahead=7,
        rank=rank,
    )


def input_terms_call(parts, weight, line=None):
    keys = parts[0].shape[0]
    rows = keys // 2
    _, width, half = weight.shape

    def body(*refs):
        ins, w, near, far = refs[:-3], refs[-3], refs[-2], refs[-1]
        for i, out in enumerate((near, far)):
            acc = 0.0
            for c in range(3):
                of = slice(c * PAIR, (c + 1) * PAIR)
                d = jnp.concatenate([part[i * rows : (i + 1) * rows, of] for part in ins], axis=1)
                acc = acc + dot(d, w[c], NT)
            out[...] = acc.astype(out.dtype)

    return call(
        body,
        (),
        [VM] * (len(parts) + 1),
        [VM] * 2,
        [shape_of((rows, width), F32), shape_of((rows, width), BF16)],
        (*parts, weight),
        line=line,
        room=12,
    )


def end_call(tokens, d_middle, near, far, vecs, line=None):
    rows, width = tokens.shape

    def body(tok, dm, dn, df, vec, grad_out, sum_out):
        normed, inverse = norm_parts(tok[...].astype(F32))
        d_in = dn[...] + df[...].astype(F32)
        grad_out[...] = (dm[...] + norm_back(d_in * vec[0:1], normed, inverse)).astype(BF16)
        sum_out[0:1] = total(d_in)
        sum_out[1:2] = total(d_in * normed)
        sum_out[2:8] = jnp.zeros((6, width), F32)

    return call(
        body,
        (),
        [VM] * 5,
        [VM] * 2,
        [pltpu.HBM((rows, width), BF16), shape_of((8, width), F32)],
        (tokens, d_middle, near, far, vecs),
        line=line,
    )


def swap(value):
    return lax.ppermute(value, "tensor", [(0, 1), (1, 0)])


def bit_swap(value, bit, order_by_core):
    pairs = []
    for place in range(lax.axis_size("dp")):
        for core in range(2):
            use = bit ^ core if order_by_core else bit
            pairs.append((place * 2 + core, (place ^ (1 << use)) * 2 + core))
    return lax.ppermute(value, ("dp", "tensor"), pairs)


def pick(value, index):
    return lax.dynamic_index_in_dim(value, index, 0, keepdims=False)


def join(mine, other, index):
    return jnp.where(index == 0, jnp.stack([mine, other]), jnp.stack([other, mine]))


def bit_count():
    return lax.axis_size("dp").bit_length() - 1


def pack_call(blocks, bit, line=None):
    width, size = blocks[0].shape

    def body(b, one, two, three, four, send, keep):
        def put(low, high):
            low[:, :size], low[:, size:] = one[...], two[...]
            high[:, :size], high[:, size:] = three[...], four[...]

        pl.when(b[0] == 0)(lambda: put(keep, send))
        pl.when(b[0] != 0)(lambda: put(send, keep))

    return call(
        body,
        (),
        [SM] + [VM] * 4,
        [VM, VM],
        [shape_of((width, 2 * size), BF16)] * 2,
        (bit, *blocks),
        line=line,
    )


def shared_call(end_sums, turn_sums, out_sums, down_sums, vecs, line=None):
    width = vecs.shape[1]

    def body(ends, turn, out, down, vec, rows):
        rows[0:1] = ends[0:1]
        rows[1:2] = ends[1:2] * vec[7:8]
        rows[2:4] = turn[0:2]
        rows[4:5] = turn[2:3] * vec[8:9]
        rows[5:6] = out[0:1]
        rows[6:7] = ends[1:2] * vec[9:10]
        rows[7:8] = turn[2:3] * vec[10:11]
        rows[8:9] = down[...]
        rows[9:16] = jnp.zeros((7, width), F32)

    return call(
        body,
        (),
        [VM] * 5,
        VM,
        shape_of((16, width), F32),
        (end_sums, turn_sums, out_sums, down_sums, vecs),
        line=line,
    )


def small_call(mine, other, b_up_sums, b_qkv_sums, line=None):
    width = mine.shape[1]
    half = width // 2

    def body(one, two, up_0, up_1, qkv_0, qkv_1, qkv_2, rows):
        rows[...] = jnp.concatenate(
            [
                (one[...] + two[...])[:9],
                up_0[...],
                up_1[...],
                jnp.concatenate([qkv_0[...], qkv_1[...]], axis=1),
                jnp.concatenate([qkv_2[...], jnp.zeros((1, half), F32)], axis=1),
                jnp.zeros((3, width), F32),
            ],
            axis=0,
        ).astype(BF16)

    return call(
        body,
        (),
        [VM] * 7,
        VM,
        shape_of((16, width), BF16),
        (mine, other, *b_up_sums, *b_qkv_sums),
        line=line,
    )


def append_call(mine, other, line=None):
    rows, width = mine.shape

    def body(one, two, out):
        out[:rows] = one[...]
        out[rows:] = two[...]

    return call(
        body, (), [VM, VM], VM, shape_of((2 * rows, width), BF16), (mine, other), line=line
    )


def split_add(mine, other, bit, line=None):
    rows, width = mine.shape

    def body(b, one, two, send, keep):
        field = (one[...].astype(F32) + two[...].astype(F32)).astype(BF16)
        low, high = field[: rows // 2], field[rows // 2 :]

        @pl.when(b[0] == 0)
        def _():
            keep[...] = low
            send[...] = high

        @pl.when(b[0] != 0)
        def _():
            send[...] = low
            keep[...] = high

    return call(
        body,
        (),
        [SM, VM, VM],
        [VM, VM],
        [shape_of((rows // 2, width), BF16)] * 2,
        (bit, mine, other),
        line=line,
    )


def plain_add(mine, other, line=None):
    def body(one, two, out):
        out[...] = (one[...].astype(F32) + two[...].astype(F32)).astype(BF16)

    return call(
        body, (), [VM, VM], VM, shape_of(mine.shape, BF16), (mine, other), line=line
    )


def stack_halves(mine, other, bit, line=None):
    rows, width = mine.shape

    def body(b, one, two, out):
        out[pl.ds(pl.multiple_of(b[0] * rows, rows), rows)] = one[...]
        out[pl.ds(pl.multiple_of((1 - b[0]) * rows, rows), rows)] = two[...]

    return call(
        body,
        (),
        [SM, VM, VM],
        VM,
        shape_of((2 * rows, width), BF16),
        (bit, mine, other),
        line=line,
    )


def unpack_call(mine, other, bit, before, units, at, line=None):
    width = mine.shape[0]
    size = mine.shape[1]

    def body(b, one, two, *rest):
        down_out, up_out = rest[-2:]

        @pl.when(b[0] == 0)
        def _():
            down_out[...] = one[...].astype(F32)
            up_out[...] = two[...].astype(F32)

        @pl.when(b[0] != 0)
        def _():
            down_out[...] = two[...].astype(F32)
            up_out[...] = one[...].astype(F32)

    extra = [pl.BlockSpec(memory_space=pl.ANY)] * len(before)
    return call(
        body,
        (1,),
        [SM, whole(mine.shape), whole(mine.shape)] + extra,
        [
            pl.BlockSpec((size, width), lambda i: (at, 0)),
            pl.BlockSpec((width, size), lambda i: (0, at)),
        ],
        [pltpu.HBM((units, width), F32), pltpu.HBM((width, units), F32)],
        (bit, mine, other) + tuple(far_core(x) for x in before),
        line=line,
        aliases={3: 0, 4: 1} if before else None,
        room=16,
    )


def unpack_last_call(mine, other, bit, line=None):
    width, size = mine.shape
    half = size // 2

    def body(b, one, two, qkv_out, out_out):
        def put(low, high):
            for j, block in enumerate((low[:, :half], low[:, half:], high[:, :half])):
                for c in range(3):
                    qkv_out[c, :, j * PAIR : (j + 1) * PAIR] = block[:, c * PAIR : (c + 1) * PAIR].astype(F32)
            out_out[:, :half] = high[:half, half:].astype(F32)
            out_out[:, half:] = high[half:, half:].astype(F32)

        pl.when(b[0] == 0)(lambda: put(one, two))
        pl.when(b[0] != 0)(lambda: put(two, one))

    return call(
        body,
        (),
        [SM, VM, VM],
        [VM, VM],
        [pltpu.HBM((3, width, half), F32), pltpu.HBM((half, width), F32)],
        (bit, mine, other),
        line=line,
    )


def reduce_steps(send, keep, bits, halve, line):
    first, second, third = bits
    other = bit_swap(send, 0, True)
    yield other
    send, keep = split_add(keep, other, second, line)
    other = bit_swap(send, 1, True)
    yield other
    if halve:
        send, keep = split_add(keep, other, third, line)
        other = bit_swap(send, 2, False)
        yield other
        mine = plain_add(keep, other, line)
    else:
        mine = plain_add(keep, other, line)
        other = bit_swap(mine, 2, False)
        yield other
        mine = plain_add(mine, other, line)
    for bit in range(3, bit_count()):
        other = bit_swap(mine, bit, False)
        yield other
        mine = plain_add(mine, other, line)
    if halve:
        other = bit_swap(mine, 2, False)
        yield other
        mine = stack_halves(mine, other, third, line)
    other = bit_swap(mine, 1, True)
    yield other
    mine = stack_halves(mine, other, second, line)
    yield mine, bit_swap(mine, 0, True)


class Gather:
    def __init__(self, value, line):
        self.line = line
        self.value = value
        self.bit = 0
        self.other = bit_swap(value, 0, False)

    def go(self):
        if self.bit < bit_count():
            self.value = append_call(self.value, self.other, self.line)
            self.bit += 1
            if self.bit < bit_count():
                self.other = bit_swap(self.value, self.bit, False)

    def all(self):
        while self.bit < bit_count():
            self.go()
        return self.value


def tree_sum(value):
    while value.shape[0] > 1:
        value = value.reshape((-1, 2) + value.shape[1:])
        value = value[:, 0] + value[:, 1]
    return value[0]


class Line:
    def __init__(self):
        self.turn = jnp.zeros((8, 128), F32)

    def go(self):
        raise ValueError("unknown step")


class Group:
    def __init__(self, name, send, keep, bits, line, halve=True):
        self.name = name
        self.steps = reduce_steps(send, keep, bits, halve, line)
        with jax.named_scope(name):
            self.waiting = next(self.steps)

    def go(self):
        if not isinstance(self.waiting, tuple):
            self.waiting = next(self.steps)

    def halves(self):
        while not isinstance(self.waiting, tuple):
            self.go()
        return self.waiting


def shards(
    tokens,
    temb,
    lengths,
    w_mod,
    b_mod,
    gain_attn,
    query_key_value_weight,
    b_qkv,
    attention_output_weight,
    gain_mlp,
    up_weight,
    b_up,
    down_weight,
    b_down,
    cotangent,
):
    tokens, cotangent, length = tokens[0], cotangent[0], lengths[0]
    rows, width = tokens.shape
    core = lax.axis_index("tensor")
    place = lax.axis_index("dp")
    bits = [
        jnp.reshape((place >> b) & 1, (1,)).astype(jnp.int32) for b in (core, 1 - core, jnp.int32(2))
    ]
    half = width // 2
    start = core * rows
    counts = jnp.clip(jnp.stack([length - start, length - (rows - start)]), 0, rows)

    qkv_weight = jnp.swapaxes(query_key_value_weight, 0, 1)
    embed_part = lax.all_to_all(temb, "dp", split_axis=1, concat_axis=0, tiled=True)
    later, later_start, b_qkv, b_up, b_mod, b_down, gain_attn, gain_mlp, embed_part = lax.optimization_barrier(
        (tokens, start, b_qkv, b_up, b_mod, b_down, gain_attn, gain_mlp, embed_part)
    )
    qkv_bias = b_qkv.reshape(3, 1, half).astype(F32)
    up_bias = b_up.reshape(1, -1).astype(F32)
    normed_attn, _ = norm_parts(later.astype(F32))
    cosine, sine = rotary_tables(later_start, rows)
    mod_terms = jnp.dot(embed_part, w_mod, preferred_element_type=F32)
    mod_terms = lax.all_to_all(mod_terms, "dp", split_axis=0, concat_axis=0, tiled=True)
    mod_terms, cosine, sine, normed_attn, qkv_bias, up_bias = lax.optimization_barrier(
        (mod_terms, cosine, sine, normed_attn, qkv_bias, up_bias)
    )
    modulation = jnp.sum(mod_terms, axis=0) + b_mod.astype(F32)
    shift_attn, scale_attn, gate_attn, shift_mlp, scale_mlp, gate_mlp = modulation.reshape(6, width)
    gain_attn = gain_attn.astype(F32)
    gain_mlp = gain_mlp.astype(F32)
    vecs = jnp.stack(
        [
            gain_attn * (1.0 + scale_attn),
            shift_attn,
            gate_attn,
            gain_mlp * (1.0 + scale_mlp),
            shift_mlp,
            gate_mlp,
            b_down.astype(F32),
            gain_attn,
            gain_mlp,
            1.0 + scale_attn,
            1.0 + scale_mlp,
        ]
    )

    attn_in, x_near = input_call(normed_attn, vecs)
    attn_in_far = swap(attn_in)
    g_mlp, down_sums = upstream_call(counts, cotangent, vecs)
    g_mlp_far = swap(g_mlp)
    e, o_t, inv, branch_near, branch_far, qkv, trig = attend_call(
        counts, attn_in, attn_in_far, qkv_weight, qkv_bias, cosine, sine, attention_output_weight
    )
    attn_branch, fed = middle_call(tokens, branch_near, swap(branch_far), vecs)
    fed_far = swap(fed)
    units = up_weight.shape[1]
    size = units // 2
    line = Line()
    b_up_sums, groups, made = [], {}, {}
    before = ()
    for part, name in enumerate(("mlp_first", "mlp_second")):
        send, keep, b_up_sum, *before = mlp_call(
            part * size, size, bits[0], fed, fed_far, g_mlp, g_mlp_far, up_weight, down_weight, up_bias, before, line
        )
        groups[name] = Group(name, send, keep, bits, line)
        b_up_sums.append(b_up_sum)
    made["d_near"], d_far, made["b_near"], b_far = before
    made["d_far"] = swap(d_far)
    made["b_far"] = swap(b_far)

    def turn():
        made["d_middle"], g_attn, made["turn_sums"] = turn_call(
            counts, tokens, cotangent, attn_branch, made["d_near"], made["d_far"], vecs, line
        )
        made["g"] = (g_attn, swap(g_attn))
        made["x_far"] = swap(lax.optimization_barrier((x_near, g_attn))[0])

    def back():
        send, keep, sums, *made["d_alls"] = attend_back_call(
            bits[0], *made["g"], attention_output_weight, qkv, e, o_t, inv, trig, cosine, sine, x_near, made["x_far"], line
        )
        made["b_qkv"] = [sums[n : n + 1] for n in range(sums.shape[0])]
        groups["projections"] = Group("projections", send, keep, bits, line)

    def d_attn_in():
        made["a_near"], a_far = input_terms_call(made["d_alls"], qkv_weight, line)
        made["a_far"] = swap(a_far)

    def finish():
        made["output"], made["out_sums"] = finish_call(
            counts, tokens, cotangent, attn_branch, made["b_near"], made["b_far"], vecs, line
        )

    def end():
        made["grad_tokens"], made["end_sums"] = end_call(
            tokens, made["d_middle"], made["a_near"], made["a_far"], vecs, line
        )

    def share():
        shared = shared_call(made["end_sums"], made["turn_sums"], made["out_sums"], down_sums, vecs, line)
        made["shared"] = (shared, swap(shared))

    def small():
        rows = small_call(*made["shared"], b_up_sums, made["b_qkv"], line)
        groups["small"] = Gather(rows, line)

    def unpack(at, name):
        made["totals"] = unpack_call(*groups[name].halves(), bits[0], made.get("totals", ()), units, at, line)

    acts = [turn, back, d_attn_in, finish, end, share, small]
    acts = {act.__name__: act for act in acts}
    gather = acts.pop("small")
    acts["begin"] = gather
    acts["unpack_first"] = lambda: unpack(0, "mlp_first")
    acts["unpack_second"] = lambda: unpack(1, "mlp_second")
    for word in ORDER:
        with jax.named_scope(word):
            acts.get(word, groups.get(word, line).go)()
    groups["projections"].halves()
    every = groups["small"].all().reshape(-1, 16, width)
    grad_mod_all = every[:, :6].reshape(-1, 6 * width)
    embed_order = lax.iota(jnp.int32, every.shape[0]) ^ place
    embed_here = jnp.take(embed_part, embed_order, axis=0)
    grad_w_mod = dot(embed_here, grad_mod_all, TN)
    embed_terms = jnp.take(dot(grad_mod_all, w_mod, NT), embed_order, axis=0)
    grad_temb = lax.all_to_all(embed_terms, "dp", split_axis=0, concat_axis=1, tiled=True)
    sums = tree_sum(every.astype(F32))
    output, grad_tokens, totals = made["output"], made["grad_tokens"], made["totals"]
    down_total, up_total = totals
    qkv_total, out_total = unpack_last_call(*groups["projections"].halves(), bits[0], line)
    b_up_total = sums[9:11].reshape(-1)
    b_qkv_total = sums[11:13].reshape(-1)[: 9 * PAIR].reshape(3, 3, PAIR)
    return (
        output[None],
        grad_tokens[None],
        grad_temb,
        grad_w_mod,
        sums[:6].reshape(-1),
        sums[6],
        jnp.swapaxes(qkv_total, 0, 1),
        jnp.swapaxes(b_qkv_total, 0, 1).reshape(3, half),
        out_total,
        sums[7],
        up_total,
        b_up_total,
        down_total,
        sums[8],
    )


def solution(mesh):
    return jax.shard_map(
        shards,
        mesh=mesh,
        in_specs=(
            P("dp", "tensor", None),
            P("dp", None),
            P("dp"),
            P("dp", None),
            P(),
            P(),
            P(None, None, "tensor"),
            P(None, "tensor"),
            P("tensor", None),
            P(),
            P(None, "tensor"),
            P("tensor"),
            P("tensor", None),
            P(),
            P("dp", "tensor", None),
        ),
        out_specs=(
            P("dp", "tensor", None),
            P("dp", "tensor", None),
            P("dp", None),
            P("dp", None),
            P(),
            P(),
            P(None, None, "tensor"),
            P(None, "tensor"),
            P("tensor", None),
            P(),
            P(None, "tensor"),
            P("tensor"),
            P("tensor", None),
            P(),
        ),
        check_vma=False,
    )
```

time: 293 us -> 259 us (0.88)
  local copies, waits for them, and re-layouts: 37.4 us -> 16 us
  starting transfers between devices: 46.1 us -> 37.3 us
  waiting for transfers between devices: 97.2 us -> 93 us
    unnamed x131 -> x51, local copies, waits for them, and re-layouts: 30.8 us -> 9.34 us
    ppermute x25, waiting for transfers between devices: 79.9 us -> 71.4 us  [bit_swap(): return lax.ppermute(value, ('dp', 'tensor'), pairs)]
    ppermute x25, starting transfers between devices: 27.7 us -> 20.5 us  [bit_swap(): return lax.ppermute(value, ('dp', 'tensor'), pairs)]
    ppermute x9 -> x10, waiting for transfers between devices: 4.1 us -> 9.19 us  [swap(): return lax.ppermute(value, 'tensor', [(0, 1), (1, 0)])]
    all_to_all x1, waiting for transfers between devices: 3.08 us -> 0.01 us  [shards(): lax.all_to_all(embed_terms, 'dp', split_axis=0, concat_axis=1, tiled=True)]
    pallas_call x45 -> x38, Pallas kernels: 98.9 us -> 100 us  [call(): pl.pallas_call(wrapped, grid=grid, in_specs=in_specs, out_specs=out_specs...]
  transfers between devices with their start and end apart: 37 -> 38, of which waited for: 19 -> 19; matrix products, arithmetic and copies ran while one was open for 5% -> 4% of each run, Pallas kernels for 17% -> 27%
where the time goes in v1:
time: 259 us; the launch traced here: 257 us
  Pallas kernels  100 us (39%)
  waiting for transfers between devices  93 us (36%)
  starting transfers between devices  37.3 us (14%)
  local copies, waits for them, and re-layouts  16 us (6%)
  other arithmetic  6.41 us (2%)
    pallas_call x38, Pallas kernels, call(): pl.pallas_call(wrapped, grid=grid, in_specs=in_specs, out_specs=out_specs...  100 us
    ppermute x25, waiting for transfers between devices, bit_swap(): return lax.ppermute(value, ('dp', 'tensor'), pairs)  71.4 us
    ppermute x25, starting transfers between devices, bit_swap(): return lax.ppermute(value, ('dp', 'tensor'), pairs)  20.5 us
    unnamed x51, local copies, waits for them, and re-layouts  9.34 us
    ppermute x10, waiting for transfers between devices, swap(): return lax.ppermute(value, 'tensor', [(0, 1), (1, 0)])  9.19 us
    all_to_all x1, starting transfers between devices, shards(): lax.all_to_all(temb, 'dp', split_axis=1, concat_axis=0, tiled=True)  8.31 us
    all_to_all x1, waiting for transfers between devices, shards(): lax.all_to_all(temb, 'dp', split_axis=1, concat_axis=0, tiled=True)  7.18 us
    all_to_all x1, waiting for transfers between devices, shards(): lax.all_to_all(mod_terms, 'dp', split_axis=0, concat_axis=0, tiled=True)  5.19 us
  transfers between devices with their start and end apart: 38, of which 19 were waited for; matrix products, arithmetic and copies ran while one was open for 4% of the time, Pallas kernels for 27%

profile of v1, /device:TPU:0, one launch (start us, length us, event | category | flops | bytes accessed | tf_op | source)
XLA Modules:
  0.0 256.7 jit_solution(11398487188923906904)
XLA Ops:
  2.2 8.3 %all-to-all-start = ((bf16[1,16,48]{2,0,1:T(2,128)(2,1)}), bf16[1,16,48]{2,0,1:T(2,128)(2,1)S(1)}, u32[]{:S(2)}, u32[]{:S(2)}) async-start(bf16[1,16,48]{2,0,1:T(2,128)(2,1)} %all_to_all.38), calls=%async_computation | async-start | bytes 16384 | tf_op jit(solution)/shard_map/all_to_all | solution.py:976
  10.5 7.2 %all-to-all-done = bf16[1,16,48]{2,0,1:T(2,128)(2,1)S(1)} async-done(((bf16[1,16,48]{2,0,1:T(2,128)(2,1)}), bf16[1,16,48]{2,0,1:T(2,128)(2,1)S(1)}, u32[]{:S(2)}, u32[]{:S(2)}) %all-to-all-start) | async-done | bytes 1568 | tf_op jit(solution)/shard_map/all_to_all | solution.py:976
  18.9 3.5 %all-to-all-start.1 = ((f32[16,1,4608]{2,1,0:T(1,128)}), f32[16,1,4608]{2,1,0:T(1,128)S(1)}, u32[]{:S(2)}, u32[]{:S(2)}) async-start(f32[16,1,4608]{2,1,0:T(1,128)} %copy.38), calls=%async_computation.1 | async-start | bytes 589824 | tf_op jit(solution)/shard_map/all_to_all | solution.py:985
  23.2 3.1 %fusion.3 = (f32[1024,128]{1,0:T(8,128)}, f32[1024,128]{1,0:T(8,128)}) fusion(f32[128]{0:T(128)S(1)} %get-tuple-element.282, f32[128]{0:T(128)S(1)} %get-tuple-element.283, f32[1024]{0:T(1024)S(1)} %add_convert_fusion), kind=kLoop, calls=%fused_computation.10 | loop fusion | flops 262144 | bytes 1053696 | tf_op jit(solution)/shard_map/mul | solution.py:407
  26.6 5.2 %all-to-all-done.1 = f32[16,1,4608]{2,1,0:T(1,128)S(1)} async-done(((f32[16,1,4608]{2,1,0:T(1,128)}), f32[16,1,4608]{2,1,0:T(1,128)S(1)}, u32[]{:S(2)}, u32[]{:S(2)}) %all-to-all-start.1) | async-done | bytes 294944 | tf_op jit(solution)/shard_map/all_to_all | solution.py:985
  35.9 17.5 %shard_map.255 = (bf16[3,2,2,1024,512]{4,3,2,1,0:T(8,128)(2,1)}, bf16[384,1024]{1,0:T(8,128)(2,1)}, f32[3,2,1,1024]{3,2,1,0:T(1,128)S(1)}, f32[512,768]{1,0:T(8,...) custom-call(s32[2]{0:T(128)S(1)} %add_clamp_fusion.refs_0_, ...), custom_call_target="tpu_custom_call" | custom-call | tf_op jit(solution)/shard_map/pallas_call | solution.py:122
  57.8 2.5 collective-permute-done.2.refs_2_
  63.6 8.6 %shard_map.258 = (bf16[768,768]{1,0:T(8,128)(2,1)}, bf16[768,768]{1,0:T(8,128)(2,1)}, f32[1,768]{1,0:T(1,128)S(1)}, bf16[1024,768]{1,0:T(8,128)(2,1)S(1)}, bf16[...) custom-call(s32[1]{0:T(128)} %bitcast.7.refs_0_, bf16[512,768]{1,0:T(8,128)(2,1)} %get-tuple-element.157.refs_1_, ...), custom_call_target="tpu_custom_call" | custom-call | tf_op jit(solution)/shard_map/pallas_call | solution.py:122
  73.1 13.8 %shard_map.259 = (bf16[768,768]{1,0:T(8,128)(2,1)}, bf16[768,768]{1,0:T(8,128)(2,1)}, f32[1,768]{1,0:T(1,128)S(1)}, f32[512,768]{1,0:T(8,128)S(1)}, bf16[512,768...) custom-call(s32[1]{0:T(128)} %bitcast.7.refs_0_, ...), custom_call_target="tpu_custom_call" | custom-call | tf_op jit(solution)/shard_map/pallas_call | solution.py:122
  88.1 3.7 %collective-permute-start.7 = (bf16[768,768]{1,0:T(8,128)(2,1)}, bf16[768,768]{1,0:T(8,128)(2,1)}, u32[]{:S(2)}, u32[]{:S(2)}) collective-permute-start(bf16[768,768]{1,0:T(8,128)(2,1)} %get-tuple-element.171), channel_id=1, source_target_pairs={{0,2},{1,5},{2,0},{3,7},{4,6},{5,1},{6,4},{7,3},{8,10},{9,13},{10,... | collective-permute-start | bytes 3538952 | tf_op jit(solution)/shard_map/mlp_second/ppermute | solution.py:647
  93.1 3.1 %mlp_first.6 = (bf16[384,768]{1,0:T(8,128)(2,1)}, bf16[384,768]{1,0:T(8,128)(2,1)S(1)}, f32[8,128]{1,0:T(8,128)S(1)}) custom-call(s32[1]{0:T(128)} %bitcast.9.refs_0_, bf16[768,768]{1,0:T(8,128)(2,1)S(1)} %copy-done.13, bf16[768,768]{1,0:T(8,128)(2,1)} %collective-permute-done.5.refs_2_, f32[8,128]{1,0:T(8,128)S(1)} %get-tuple-element.167.refs_3_), custom_call_target="tpu_custom_call" | custom-call | flops 1000000000 | tf_op jit(solution)/shard_map/mlp_first/pallas_call | solution.py:122
  96.2 3.6 %turn.1 = (f32[512,768]{1,0:T(8,128)}, bf16[512,768]{1,0:T(8,128)(2,1)}, f32[8,768]{1,0:T(8,128)S(1)}, f32[8,128]{1,0:T(8,128)S(1)}) custom-call(s32[2]{0:T(128)S(1)} %add_clamp_fusion.refs_0_, bf16[512,768]{1,0:T(8,128)(2,1)S(1)} %bitcast.59, bf16[512,768]{1,0:T(8,128)(2,1)S(1)} %bitcast.65, f32[512,768]{1,0:T(8,128)S(1)} %copy-done.6, ...), custom_call_target="tpu_custom_call" | custom-call | flops 1000000000 | tf_op jit(solution)/shard_map/turn/pallas_call | solution.py:122
  102.4 2.2 collective-permute-done.10.refs_10_
  104.7 24.5 %back.1 = (bf16[768,768]{1,0:T(8,128)(2,1)S(1)}, bf16[768,768]{1,0:T(8,128)(2,1)S(1)}, f32[3,384]{1,0:T(4,128)S(1)}, bf16[1024,384]{1,0:T(8,128)(2,1)S(1)}, bf16...) custom-call(s32[1]{0:T(128)} %bitcast.7.refs_0_, ...), custom_call_target="tpu_custom_call" | custom-call | flops 1000000000 | tf_op jit(solution)/shard_map/back/pallas_call | solution.py:122
  134.8 2.7 %d_attn_in.1 = (f32[512,768]{1,0:T(8,128)S(1)}, bf16[512,768]{1,0:T(8,128)(2,1)S(1)}, f32[8,128]{1,0:T(8,128)S(1)}) custom-call(bf16[1024,384]{1,0:T(8,128)(2,1)S(1)} %get-tuple-element.190.refs_0_, bf16[1024,384]{1,0:T(8,128)(2,1)S(1)} %get-tuple-element.191.refs_1_, bf16[1024,384]{1,0:T(8,128)(2,1)S(1)} %get-tuple-element.192.refs_2_, ...), custom_call_target="tpu_custom_call" | custom-call | flops 1000000000 | tf_op jit(solution)/shard_map/d_attn_in/pallas_call | solution.py:122
  137.7 9.7 %collective-permute-done.12.refs_2_ = bf16[384,768]{1,0:T(8,128)(2,1)S(1)} collective-permute-done((bf16[384,768]{1,0:T(8,128)(2,1)S(1)}, bf16[384,768]{1,0:T(8,128)(2,1)S(1)}, u32[]{:S(2)}, u32[]{:S(2)}) %collective-permute-start.12) | collective-permute-done | bytes 589856 | tf_op jit(solution)/shard_map/mlp_second/ppermute | solution.py:647
  149.7 2.2 finish.1
  151.9 2.2 end.1
  157.5 5.5 %collective-permute-done.18.refs_1_ = bf16[192,768]{1,0:T(8,128)(2,1)S(1)} collective-permute-done((bf16[192,768]{1,0:T(8,128)(2,1)S(1)}, bf16[192,768]{1,0:T(8,128)(2,1)S(1)}, u32[]{:S(2)}, u32[]{:S(2)}) %collective-permute-start.18) | collective-permute-done | bytes 294944 | tf_op jit(solution)/shard_map/mlp_first/ppermute | solution.py:647
  163.2 3.4 %collective-permute-done.17.refs_2_ = bf16[384,768]{1,0:T(8,128)(2,1)S(1)} collective-permute-done((bf16[384,768]{1,0:T(8,128)(2,1)S(1)}, bf16[384,768]{1,0:T(8,128)(2,1)S(1)}, u32[]{:S(2)}, u32[]{:S(2)}) %collective-permute-start.17) | collective-permute-done | bytes 589856 | tf_op jit(solution)/shard_map/projections/ppermute | solution.py:647
  167.0 4.3 %collective-permute-done.22.refs_2_ = bf16[192,768]{1,0:T(8,128)(2,1)S(1)} collective-permute-done((bf16[192,768]{1,0:T(8,128)(2,1)S(1)}, bf16[192,768]{1,0:T(8,128)(2,1)S(1)}, u32[]{:S(2)}, u32[]{:S(2)}) %collective-permute-start.22) | collective-permute-done | bytes 294944 | tf_op jit(solution)/shard_map/mlp_first/ppermute | solution.py:647
  171.9 2.5 collective-permute-start.19
  174.3 11.5 %collective-permute-done.21.refs_1_ = bf16[192,768]{1,0:T(8,128)(2,1)S(1)} collective-permute-done((bf16[192,768]{1,0:T(8,128)(2,1)S(1)}, bf16[192,768]{1,0:T(8,128)(2,1)S(1)}, u32[]{:S(2)}, u32[]{:S(2)}) %collective-permute-start.21) | collective-permute-done | bytes 294944 | tf_op jit(solution)/shard_map/mlp_second/ppermute | solution.py:647
  189.3 10.4 %collective-permute-done.24.refs_1_ = bf16[192,768]{1,0:T(8,128)(2,1)S(1)} collective-permute-done((bf16[192,768]{1,0:T(8,128)(2,1)S(1)}, bf16[192,768]{1,0:T(8,128)(2,1)S(1)}, u32[]{:S(2)}, u32[]{:S(2)}) %collective-permute-start.24) | collective-permute-done | bytes 294944 | tf_op jit(solution)/shard_map/projections/ppermute | solution.py:647
  205.4 2.5 unpack_first.1
  207.9 5.4 %collective-permute-done.29.refs_2_ = bf16[192,768]{1,0:T(8,128)(2,1)S(1)} collective-permute-done((bf16[192,768]{1,0:T(8,128)(2,1)S(1)}, bf16[192,768]{1,0:T(8,128)(2,1)S(1)}, u32[]{:S(2)}, u32[]{:S(2)}) %collective-permute-start.29) | collective-permute-done | bytes 294944 | tf_op jit(solution)/shard_map/projections/ppermute | solution.py:647
  216.7 9.9 %collective-permute-done.31.refs_1_ = bf16[128,768]{1,0:T(8,128)(2,1)S(1)} collective-permute-done((bf16[128,768]{1,0:T(8,128)(2,1)S(1)}, bf16[128,768]{1,0:T(8,128)(2,1)S(1)}, u32[]{:S(2)}, u32[]{:S(2)}) %collective-permute-start.31) | collective-permute-done | bytes 196640 | tf_op jit(solution)/shard_map/small/ppermute | solution.py:647
  229.8 3.5 %all-to-all-start.2 = ((f32[16,1,48]{2,1,0:T(1,128)}), f32[16,1,48]{2,1,0:T(1,128)S(1)}, u32[]{:S(2)}, u32[]{:S(2)}) async-start(f32[16,1,48]{2,1,0:T(1,128)} %bitcast.15), calls=%async_computation.2 | async-start | bytes 16384 | tf_op jit(solution)/shard_map/all_to_all | solution.py:1088
  233.5 2.3 projections.11
  243.3 2.5 unpack_second.1
  245.8 6.6 %collective-permute-done.33.refs_2_ = bf16[768,768]{1,0:T(8,128)(2,1)} collective-permute-done((bf16[768,768]{1,0:T(8,128)(2,1)}, bf16[768,768]{1,0:T(8,128)(2,1)}, u32[]{:S(2)}, u32[]{:S(2)}) %collective-permute-start.33) | collective-permute-done | bytes 1179680 | tf_op jit(solution)/shard_map/projections/ppermute | solution.py:647
  252.4 4.1 %shard_map.260 = (f32[3,768,384]{2,1,0:T(8,128)}, f32[384,768]{1,0:T(8,128)}, f32[8,128]{1,0:T(8,128)}) custom-call(s32[1]{0:T(128)} %bitcast.7.refs_0_, bf16[768,768]{1,0:T(8,128)(2,1)} %get-tuple-element.254.refs_1_, bf16[768,768]{1,0:T(8,128)(2,1)} %collective-permute-done.33.refs_2_, f32[8,128]{1,0:T(8,128)S(1)} %get-tuple-element.259.refs_3_), custom_call_target="tpu_custom_call" | custom-call | flops 1000000000 | tf_op jit(solution)/shard_map/pallas_call | solution.py:122
  (191 shorter events, 56.3 us)
Async XLA Ops:
  2.2 15.5 %all-to-all-start = ((bf16[1,16,48]{2,0,1:T(2,128)(2,1)}), bf16[1,16,48]{2,0,1:T(2,128)(2,1)S(1)}, u32[]{:S(2)}, u32[]{:S(2)}) async-start(bf16[1,16,48]{2,0,1:T(2,128)(2,1)} %all_to_all.38), calls=%async_computation | async-start | bytes 16384 | tf_op jit(solution)/shard_map/all_to_all | solution.py:976
  18.9 12.8 %all-to-all-start.1 = ((f32[16,1,4608]{2,1,0:T(1,128)}), f32[16,1,4608]{2,1,0:T(1,128)S(1)}, u32[]{:S(2)}, u32[]{:S(2)}) async-start(f32[16,1,4608]{2,1,0:T(1,128)} %copy.38), calls=%async_computation.1 | async-start | bytes 589824 | tf_op jit(solution)/shard_map/all_to_all | solution.py:985
  72.2 19.6 %collective-permute-start.5 = (bf16[768,768]{1,0:T(8,128)(2,1)}, bf16[768,768]{1,0:T(8,128)(2,1)}, u32[]{:S(2)}, u32[]{:S(2)}) collective-permute-start(bf16[768,768]{1,0:T(8,128)(2,1)} %get-tuple-element.166), channel_id=1, source_target_pairs={{0,2},{1,5},{2,0},{3,7},{4,6},{5,1},{6,4},{7,3},{8,10},{9,13},{10,... | collective-permute-start | bytes 3538952 | tf_op jit(solution)/shard_map/mlp_first/ppermute | solution.py:647
  88.1 8.1 %collective-permute-start.8 = (bf16[512,768]{1,0:T(8,128)(2,1)}, bf16[512,768]{1,0:T(8,128)(2,1)S(1)}, u32[]{:S(2)}, u32[]{:S(2)}) collective-permute-start(bf16[512,768]{1,0:T(8,128)(2,1)} %get-tuple-element.173), channel_id=1, source_target_pairs={{0,1},{1,0},{2,3},{3,2},{4,5},{5,4},{6,7},{7,6},{8,9},{9,8},{10,11... | collective-permute-start | bytes 2359304 | tf_op jit(solution)/shard_map/ppermute | solution.py:638
  88.1 41.1 %collective-permute-start.7 = (bf16[768,768]{1,0:T(8,128)(2,1)}, bf16[768,768]{1,0:T(8,128)(2,1)}, u32[]{:S(2)}, u32[]{:S(2)}) collective-permute-start(bf16[768,768]{1,0:T(8,128)(2,1)} %get-tuple-element.171), channel_id=1, source_target_pairs={{0,2},{1,5},{2,0},{3,7},{4,6},{5,1},{6,4},{7,3},{8,10},{9,13},{10,... | collective-permute-start | bytes 3538952 | tf_op jit(solution)/shard_map/mlp_second/ppermute | solution.py:647
  99.9 4.7 %collective-permute-start.10 = (bf16[512,768]{1,0:T(8,128)(2,1)}, bf16[512,768]{1,0:T(8,128)(2,1)}, u32[]{:S(2)}, u32[]{:S(2)}) collective-permute-start(bf16[512,768]{1,0:T(8,128)(2,1)} %get-tuple-element.182.refs_9_), channel_id=1, source_target_pairs={{0,1},{1,0},{2,3},{3,2},{4,5},{5,4},{6,7},{7,6},{8,9},{9,8},{10,11... | collective-permute-start | bytes 2359304 | tf_op jit(solution)/shard_map/turn/ppermute | solution.py:638
  100.3 32.9 %collective-permute-start.6 = (bf16[384,768]{1,0:T(8,128)(2,1)}, bf16[384,768]{1,0:T(8,128)(2,1)}, u32[]{:S(2)}, u32[]{:S(2)}) collective-permute-start(bf16[384,768]{1,0:T(8,128)(2,1)} %get-tuple-element.169), channel_id=1, source_target_pairs={{0,4},{1,3},{2,6},{3,1},{4,0},{5,7},{6,2},{7,5},{8,12},{9,11},{10,... | collective-permute-start | bytes 1769480 | tf_op jit(solution)/shard_map/mlp_first/ppermute | solution.py:647
  100.5 47.5 %collective-permute-start.4 = (bf16[512,768]{1,0:T(8,128)(2,1)}, bf16[512,768]{1,0:T(8,128)(2,1)S(1)}, u32[]{:S(2)}, u32[]{:S(2)}) collective-permute-start(bf16[512,768]{1,0:T(8,128)(2,1)} %get-tuple-element.164), channel_id=1, source_target_pairs={{0,1},{1,0},{2,3},{3,2},{4,5},{5,4},{6,7},{7,6},{8,9},{9,8},{10,11... | collective-permute-start | bytes 2359304 | tf_op jit(solution)/shard_map/ppermute | solution.py:638
  131.2 16.2 %collective-permute-start.12 = (bf16[384,768]{1,0:T(8,128)(2,1)S(1)}, bf16[384,768]{1,0:T(8,128)(2,1)S(1)}, u32[]{:S(2)}, u32[]{:S(2)}) collective-permute-start(bf16[384,768]{1,0:T(8,128)(2,1)S(1)} %get-tuple-element.189), channel_id=1, source_target_pairs={{0,4},{1,3},{2,6},{3,1},{4,0},{5,7},{6,2},{7,5},{8,12},{9,11},{10,... | collective-permute-start | bytes 1769480 | tf_op jit(solution)/shard_map/mlp_second/ppermute | solution.py:647
  131.3 24.8 %collective-permute-start.15 = (bf16[768,768]{1,0:T(8,128)(2,1)S(1)}, bf16[768,768]{1,0:T(8,128)(2,1)S(1)}, u32[]{:S(2)}, u32[]{:S(2)}) collective-permute-start(bf16[768,768]{1,0:T(8,128)(2,1)S(1)} %get-tuple-element.213), channel_id=1, source_target_pairs={{0,2},{1,5},{2,0},{3,7},{4,6},{5,1},{6,4},{7,3},{8,10},{9,13},{10,... | collective-permute-start | bytes 3538952 | tf_op jit(solution)/shard_map/back/projections/ppermute | solution.py:647
  137.5 14.4 %collective-permute-start.13 = (bf16[512,768]{1,0:T(8,128)(2,1)S(1)}, bf16[512,768]{1,0:T(8,128)(2,1)S(1)}, u32[]{:S(2)}, u32[]{:S(2)}) collective-permute-start(bf16[512,768]{1,0:T(8,128)(2,1)S(1)} %get-tuple-element.200), channel_id=1, source_target_pairs={{0,1},{1,0},{2,3},{3,2},{4,5},{5,4},{6,7},{7,6},{8,9},{9,8},{10,11... | collective-permute-start | bytes 2359304 | tf_op jit(solution)/shard_map/d_attn_in/ppermute | solution.py:638
  137.6 10.2 %collective-permute-start.11 = (bf16[192,768]{1,0:T(8,128)(2,1)S(1)}, bf16[192,768]{1,0:T(8,128)(2,1)S(1)}, u32[]{:S(2)}, u32[]{:S(2)}) collective-permute-start(bf16[192,768]{1,0:T(8,128)(2,1)S(1)} %get-tuple-element.187), channel_id=1, source_target_pairs={{0,8},{1,9},{2,10},{3,11},{4,12},{5,13},{6,14},{7,15},{8,0},{9,1},... | collective-permute-start | bytes 884744 | tf_op jit(solution)/shard_map/mlp_first/ppermute | solution.py:647
  147.7 8.2 %collective-permute-start.16 = (bf16[192,768]{1,0:T(8,128)(2,1)S(1)}, bf16[192,768]{1,0:T(8,128)(2,1)S(1)}, u32[]{:S(2)}, u32[]{:S(2)}) collective-permute-start(bf16[192,768]{1,0:T(8,128)(2,1)S(1)} %get-tuple-element.215), channel_id=1, source_target_pairs={{0,8},{1,9},{2,10},{3,11},{4,12},{5,13},{6,14},{7,15},{8,0},{9,1},... | collective-permute-start | bytes 884744 | tf_op jit(solution)/shard_map/mlp_second/ppermute | solution.py:647
  147.9 15.0 %collective-permute-start.18 = (bf16[192,768]{1,0:T(8,128)(2,1)S(1)}, bf16[192,768]{1,0:T(8,128)(2,1)S(1)}, u32[]{:S(2)}, u32[]{:S(2)}) collective-permute-start(bf16[192,768]{1,0:T(8,128)(2,1)S(1)} %get-tuple-element.220.refs_0_), channel_id=1, source_target_pairs={{0,16},{1,17},{2,18},{3,19},{4,20},{5,21},{6,22},{7,23},{8,24},{9,... | collective-permute-start | bytes 884744 | tf_op jit(solution)/shard_map/mlp_first/ppermute | solution.py:647
  156.7 9.9 %collective-permute-start.17 = (bf16[384,768]{1,0:T(8,128)(2,1)S(1)}, bf16[384,768]{1,0:T(8,128)(2,1)S(1)}, u32[]{:S(2)}, u32[]{:S(2)}) collective-permute-start(bf16[384,768]{1,0:T(8,128)(2,1)S(1)} %get-tuple-element.219), channel_id=1, source_target_pairs={{0,4},{1,3},{2,6},{3,1},{4,0},{5,7},{6,2},{7,5},{8,12},{9,11},{10,... | collective-permute-start | bytes 1769480 | tf_op jit(solution)/shard_map/projections/ppermute | solution.py:647
  163.0 8.2 %collective-permute-start.22 = (bf16[192,768]{1,0:T(8,128)(2,1)S(1)}, bf16[192,768]{1,0:T(8,128)(2,1)S(1)}, u32[]{:S(2)}, u32[]{:S(2)}) collective-permute-start(bf16[192,768]{1,0:T(8,128)(2,1)S(1)} %get-tuple-element.228.refs_1_), channel_id=1, source_target_pairs={{0,8},{1,9},{2,10},{3,11},{4,12},{5,13},{6,14},{7,15},{8,0},{9,1},... | collective-permute-start | bytes 884744 | tf_op jit(solution)/shard_map/mlp_first/ppermute | solution.py:647
  171.3 14.8 %collective-permute-start.25 = (bf16[384,768]{1,0:T(8,128)(2,1)S(1)}, bf16[384,768]{1,0:T(8,128)(2,1)S(1)}, u32[]{:S(2)}, u32[]{:S(2)}) collective-permute-start(bf16[384,768]{1,0:T(8,128)(2,1)S(1)} %get-tuple-element.235.refs_1_), channel_id=1, source_target_pairs={{0,4},{1,3},{2,6},{3,1},{4,0},{5,7},{6,2},{7,5},{8,12},{9,11},{10,... | collective-permute-start | bytes 1769480 | tf_op jit(solution)/shard_map/mlp_first/ppermute | solution.py:647
  171.5 14.4 %collective-permute-start.21 = (bf16[192,768]{1,0:T(8,128)(2,1)S(1)}, bf16[192,768]{1,0:T(8,128)(2,1)S(1)}, u32[]{:S(2)}, u32[]{:S(2)}) collective-permute-start(bf16[192,768]{1,0:T(8,128)(2,1)S(1)} %get-tuple-element.227.refs_0_), channel_id=1, source_target_pairs={{0,16},{1,17},{2,18},{3,19},{4,20},{5,21},{6,22},{7,23},{8,24},{9,... | collective-permute-start | bytes 884744 | tf_op jit(solution)/shard_map/mlp_second/ppermute | solution.py:647
  171.5 14.5 %collective-permute-start.20 = (bf16[192,768]{1,0:T(8,128)(2,1)S(1)}, bf16[192,768]{1,0:T(8,128)(2,1)S(1)}, u32[]{:S(2)}, u32[]{:S(2)}) collective-permute-start(bf16[192,768]{1,0:T(8,128)(2,1)S(1)} %get-tuple-element.226), channel_id=1, source_target_pairs={{0,8},{1,9},{2,10},{3,11},{4,12},{5,13},{6,14},{7,15},{8,0},{9,1},... | collective-permute-start | bytes 884744 | tf_op jit(solution)/shard_map/projections/ppermute | solution.py:647
  171.9 14.2 %collective-permute-start.19 = (bf16[16,768]{1,0:T(8,128)(2,1)S(1)}, bf16[16,768]{1,0:T(8,128)(2,1)S(1)}, u32[]{:S(2)}, u32[]{:S(2)}) collective-permute-start(bf16[16,768]{1,0:T(8,128)(2,1)S(1)} %get-tuple-element.224.refs_0_), channel_id=1, source_target_pairs={{0,2},{1,3},{2,0},{3,1},{4,6},{5,7},{6,4},{7,5},{8,10},{9,11},{10,... | collective-permute-start | bytes 73736 | tf_op jit(solution)/shard_map/begin/ppermute | solution.py:647
  186.2 19.2 %collective-permute-start.30 = (bf16[768,768]{1,0:T(8,128)(2,1)S(1)}, bf16[768,768]{1,0:T(8,128)(2,1)S(1)}, u32[]{:S(2)}, u32[]{:S(2)}) collective-permute-start(bf16[768,768]{1,0:T(8,128)(2,1)S(1)} %get-tuple-element.244.refs_1_), channel_id=1, source_target_pairs={{0,2},{1,5},{2,0},{3,7},{4,6},{5,1},{6,4},{7,3},{8,10},{9,13},{10,... | collective-permute-start | bytes 3538952 | tf_op jit(solution)/shard_map/mlp_first/ppermute | solution.py:647
  187.9 11.8 %collective-permute-start.24 = (bf16[192,768]{1,0:T(8,128)(2,1)S(1)}, bf16[192,768]{1,0:T(8,128)(2,1)S(1)}, u32[]{:S(2)}, u32[]{:S(2)}) collective-permute-start(bf16[192,768]{1,0:T(8,128)(2,1)S(1)} %get-tuple-element.234.refs_0_), channel_id=1, source_target_pairs={{0,16},{1,17},{2,18},{3,19},{4,20},{5,21},{6,22},{7,23},{8,24},{9,... | collective-permute-start | bytes 884744 | tf_op jit(solution)/shard_map/projections/ppermute | solution.py:647
  188.4 13.2 %collective-permute-start.27 = (bf16[192,768]{1,0:T(8,128)(2,1)S(1)}, bf16[192,768]{1,0:T(8,128)(2,1)S(1)}, u32[]{:S(2)}, u32[]{:S(2)}) collective-permute-start(bf16[192,768]{1,0:T(8,128)(2,1)S(1)} %get-tuple-element.240.refs_1_), channel_id=1, source_target_pairs={{0,8},{1,9},{2,10},{3,11},{4,12},{5,13},{6,14},{7,15},{8,0},{9,1},... | collective-permute-start | bytes 884744 | tf_op jit(solution)/shard_map/mlp_second/ppermute | solution.py:647
  189.1 10.7 %collective-permute-start.23 = (bf16[32,768]{1,0:T(8,128)(2,1)S(1)}, bf16[32,768]{1,0:T(8,128)(2,1)S(1)}, u32[]{:S(2)}, u32[]{:S(2)}) collective-permute-start(bf16[32,768]{1,0:T(8,128)(2,1)S(1)} %get-tuple-element.233.refs_0_), channel_id=1, source_target_pairs={{0,4},{1,5},{2,6},{3,7},{4,0},{5,1},{6,2},{7,3},{8,12},{9,13},{10,... | collective-permute-start | bytes 147464 | tf_op jit(solution)/shard_map/small/ppermute | solution.py:647
  201.7 12.4 %collective-permute-start.28 = (bf16[384,768]{1,0:T(8,128)(2,1)S(1)}, bf16[384,768]{1,0:T(8,128)(2,1)S(1)}, u32[]{:S(2)}, u32[]{:S(2)}) collective-permute-start(bf16[384,768]{1,0:T(8,128)(2,1)S(1)} %get-tuple-element.242.refs_1_), channel_id=1, source_target_pairs={{0,4},{1,3},{2,6},{3,1},{4,0},{5,7},{6,2},{7,5},{8,12},{9,11},{10,... | collective-permute-start | bytes 1769480 | tf_op jit(solution)/shard_map/mlp_second/ppermute | solution.py:647
  203.3 9.9 %collective-permute-start.29 = (bf16[192,768]{1,0:T(8,128)(2,1)S(1)}, bf16[192,768]{1,0:T(8,128)(2,1)S(1)}, u32[]{:S(2)}, u32[]{:S(2)}) collective-permute-start(bf16[192,768]{1,0:T(8,128)(2,1)S(1)} %get-tuple-element.243.refs_1_), channel_id=1, source_target_pairs={{0,8},{1,9},{2,10},{3,11},{4,12},{5,13},{6,14},{7,15},{8,0},{9,1},... | collective-permute-start | bytes 884744 | tf_op jit(solution)/shard_map/projections/ppermute | solution.py:647
  203.7 11.5 %collective-permute-start.26 = (bf16[64,768]{1,0:T(8,128)(2,1)S(1)}, bf16[64,768]{1,0:T(8,128)(2,1)S(1)}, u32[]{:S(2)}, u32[]{:S(2)}) collective-permute-start(bf16[64,768]{1,0:T(8,128)(2,1)S(1)} %get-tuple-element.239.refs_0_), channel_id=1, source_target_pairs={{0,8},{1,9},{2,10},{3,11},{4,12},{5,13},{6,14},{7,15},{8,0},{9,1},... | collective-permute-start | bytes 294920 | tf_op jit(solution)/shard_map/small/ppermute | solution.py:647
  215.1 11.5 %collective-permute-start.31 = (bf16[128,768]{1,0:T(8,128)(2,1)S(1)}, bf16[128,768]{1,0:T(8,128)(2,1)S(1)}, u32[]{:S(2)}, u32[]{:S(2)}) collective-permute-start(bf16[128,768]{1,0:T(8,128)(2,1)S(1)} %get-tuple-element.249.refs_0_), channel_id=1, source_target_pairs={{0,16},{1,17},{2,18},{3,19},{4,20},{5,21},{6,22},{7,23},{8,24},{9,... | collective-permute-start | bytes 589832 | tf_op jit(solution)/shard_map/small/ppermute | solution.py:647
  215.8 17.7 %collective-permute-start.32 = (bf16[384,768]{1,0:T(8,128)(2,1)}, bf16[384,768]{1,0:T(8,128)(2,1)}, u32[]{:S(2)}, u32[]{:S(2)}) collective-permute-start(bf16[384,768]{1,0:T(8,128)(2,1)} %get-tuple-element.252.refs_1_), channel_id=1, source_target_pairs={{0,4},{1,3},{2,6},{3,1},{4,0},{5,7},{6,2},{7,5},{8,12},{9,11},{10,... | collective-permute-start | bytes 1769480 | tf_op jit(solution)/shard_map/projections/ppermute | solution.py:647
  216.2 27.0 %collective-permute-start.34 = (bf16[768,768]{1,0:T(8,128)(2,1)S(1)}, bf16[768,768]{1,0:T(8,128)(2,1)S(1)}, u32[]{:S(2)}, u32[]{:S(2)}) collective-permute-start(bf16[768,768]{1,0:T(8,128)(2,1)S(1)} %get-tuple-element.255.refs_1_), channel_id=1, source_target_pairs={{0,2},{1,5},{2,0},{3,7},{4,6},{5,1},{6,4},{7,3},{8,10},{9,13},{10,... | collective-permute-start | bytes 3538952 | tf_op jit(solution)/shard_map/mlp_second/ppermute | solution.py:647
  229.8 11.6 %all-to-all-start.2 = ((f32[16,1,48]{2,1,0:T(1,128)}), f32[16,1,48]{2,1,0:T(1,128)S(1)}, u32[]{:S(2)}, u32[]{:S(2)}) async-start(f32[16,1,48]{2,1,0:T(1,128)} %bitcast.15), calls=%async_computation.2 | async-start | bytes 16384 | tf_op jit(solution)/shard_map/all_to_all | solution.py:1088
  235.8 16.5 %collective-permute-start.33 = (bf16[768,768]{1,0:T(8,128)(2,1)}, bf16[768,768]{1,0:T(8,128)(2,1)}, u32[]{:S(2)}, u32[]{:S(2)}) collective-permute-start(bf16[768,768]{1,0:T(8,128)(2,1)} %get-tuple-element.254.refs_1_), channel_id=1, source_target_pairs={{0,2},{1,5},{2,0},{3,7},{4,6},{5,1},{6,4},{7,3},{8,10},{9,13},{10,... | collective-permute-start | bytes 3538952 | tf_op jit(solution)/shard_map/projections/ppermute | solution.py:647
  (30 other events, 158.4 us)

commit v2 on v1

--- a/solution.py
+++ b/solution.py
@@ -21,8 +21,8 @@
     "mlp_first", "turn", "back", "mlp_second", "mlp_first", "d_attn_in", "mlp_second", "mlp_first",
     "finish", "end", "share", "mlp_second", "projections", "mlp_first", "projections", "begin",
     "mlp_first", "mlp_second", "projections", "small", "mlp_first", "projections", "small",
-    "mlp_second", "unpack_first", "projections", "mlp_second", "small", "small", "projections",
-    "unpack_second",
+    "mlp_second", "unpack_first", "projections", "mlp_second", "small", "projections", "small",
+    "unpack_second", "mod_back",
 )
 LN2 = log(2.0)
 MIB = 1024 * 1024
@@ -422,6 +422,29 @@
         [VM, VM],
         [shape_of((rows, width), BF16), pltpu.HBM((rows, width), BF16)],
         (normed, vecs),
+    )
+
+
+def carry_call(after, *weights):
+    count = len(weights)
+
+    def body(*refs):
+        ins, outs, sems = refs[1 : 1 + count], refs[1 + count : -1], refs[-1]
+        copies = [pltpu.make_async_copy(a, b, sems.at[n]) for n, (a, b) in enumerate(zip(ins, outs))]
+        for copy in copies:
+            copy.start()
+        for copy in copies:
+            copy.wait()
+
+    return call(
+        body,
+        (),
+        [pl.BlockSpec(memory_space=pl.ANY)] + [HB] * count,
+        [pl.BlockSpec(memory_space=pl.ANY)] * count,
+        [shape_of(weight.shape, BF16) for weight in weights],
+        (after, *[far_core(weight) for weight in weights]),
+        [pltpu.SemaphoreType.DMA((count,))],
+        room=1,
     )
 
 
@@ -838,23 +861,29 @@
 def unpack_last_call(mine, other, bit, line=None):
     width, size = mine.shape
     half = size // 2
+    part = half // 3
 
     def body(b, one, two, qkv_out, out_out):
         def put(low, high):
-            for j, block in enumerate((low[:, :half], low[:, half:], high[:, :half])):
-                for c in range(3):
-                    qkv_out[c, :, j * PAIR : (j + 1) * PAIR] = block[:, c * PAIR : (c + 1) * PAIR].astype(F32)
-            out_out[:, :half] = high[:half, half:].astype(F32)
-            out_out[:, half:] = high[half:, half:].astype(F32)
+            for c in range(3):
+
+                @pl.when(pl.program_id(0) == c)
+                def _():
+                    for j, (block, at) in enumerate(((low, 0), (low, half), (high, 0))):
+                        of = slice(at + c * PAIR, at + (c + 1) * PAIR)
+                        qkv_out[0, :, j * PAIR : (j + 1) * PAIR] = block[:, of].astype(F32)
+                    rows = slice(c * part, (c + 1) * part)
+                    out_out[:, :half] = high[rows, half:].astype(F32)
+                    out_out[:, half:] = high[slice(half + c * part, half + (c + 1) * part), half:].astype(F32)
 
         pl.when(b[0] == 0)(lambda: put(one, two))
         pl.when(b[0] != 0)(lambda: put(two, one))
 
     return call(
         body,
-        (),
-        [SM, VM, VM],
-        [VM, VM],
+        (3,),
+        [SM, whole(mine.shape), whole(mine.shape)],
+        [pl.BlockSpec((1, width, half), lambda c: (c, 0, 0)), pl.BlockSpec((part, width), lambda c: (c, 0))],
         [pltpu.HBM((3, width, half), F32), pltpu.HBM((half, width), F32)],
         (bit, mine, other),
         line=line,
@@ -1015,6 +1044,7 @@
     )
     attn_branch, fed = middle_call(tokens, branch_near, swap(branch_far), vecs)
     fed_far = swap(fed)
+    up_weight, down_weight = carry_call(fed, up_weight, down_weight)
     units = up_weight.shape[1]
     size = units // 2
     line = Line()
@@ -1069,7 +1099,17 @@
     def unpack(at, name):
         made["totals"] = unpack_call(*groups[name].halves(), bits[0], made.get("totals", ()), units, at, line)
 
-    acts = [turn, back, d_attn_in, finish, end, share, small]
+    def mod_back():
+        every, line.turn = lax.optimization_barrier((groups["small"].all().reshape(-1, 16, width), line.turn))
+        grad_mod_all = every[:, :6].reshape(-1, 6 * width)
+        embed_order = lax.iota(jnp.int32, every.shape[0]) ^ place
+        embed_here = jnp.take(embed_part, embed_order, axis=0)
+        made["grad_w_mod"] = dot(embed_here, grad_mod_all, TN)
+        embed_terms = jnp.take(dot(grad_mod_all, w_mod, NT), embed_order, axis=0)
+        made["grad_temb"] = lax.all_to_all(embed_terms, "dp", split_axis=0, concat_axis=1, tiled=True)
+        made["sums"] = tree_sum(every.astype(F32))
+
+    acts = [turn, back, d_attn_in, finish, end, share, small, mod_back]
     acts = {act.__name__: act for act in acts}
     gather = acts.pop("small")
     acts["begin"] = gather
@@ -1079,14 +1119,7 @@
         with jax.named_scope(word):
             acts.get(word, groups.get(word, line).go)()
     groups["projections"].halves()
-    every = groups["small"].all().reshape(-1, 16, width)
-    grad_mod_all = every[:, :6].reshape(-1, 6 * width)
-    embed_order = lax.iota(jnp.int32, every.shape[0]) ^ place
-    embed_here = jnp.take(embed_part, embed_order, axis=0)
-    grad_w_mod = dot(embed_here, grad_mod_all, TN)
-    embed_terms = jnp.take(dot(grad_mod_all, w_mod, NT), embed_order, axis=0)
-    grad_temb = lax.all_to_all(embed_terms, "dp", split_axis=0, concat_axis=1, tiled=True)
-    sums = tree_sum(every.astype(F32))
+    grad_temb, grad_w_mod, sums = made["grad_temb"], made["grad_w_mod"], made["sums"]
     output, grad_tokens, totals = made["output"], made["grad_tokens"], made["totals"]
     down_total, up_total = totals
     qkv_total, out_total = unpack_last_call(*groups["projections"].halves(), bits[0], line)

time: 259 us -> 255 us (0.985)
  waiting for transfers between devices: 93 us -> 77.4 us
  starting transfers between devices: 37.3 us -> 47.9 us
  Pallas kernels: 100 us -> 108 us
  local copies, waits for them, and re-layouts: 16 us -> 9.67 us
    ppermute x25, waiting for transfers between devices: 71.4 us -> 57.7 us  [bit_swap(): return lax.ppermute(value, ('dp', 'tensor'), pairs)]
    pallas_call x38 -> x39, Pallas kernels: 100 us -> 108 us  [call(): pl.pallas_call(wrapped, grid=grid, in_specs=in_specs, out_specs=out_specs...]
    ppermute x25, starting transfers between devices: 20.5 us -> 27.1 us  [bit_swap(): return lax.ppermute(value, ('dp', 'tensor'), pairs)]
    unnamed x51 -> x43, local copies, waits for them, and re-layouts: 9.34 us -> 3.01 us
    ppermute x10, waiting for transfers between devices: 9.19 us -> 4.08 us  [swap(): return lax.ppermute(value, 'tensor', [(0, 1), (1, 0)])]
    all_to_all x1, waiting for transfers between devices: 0.01 us -> 3.24 us  [mod_back(): lax.all_to_all(embed_terms, 'dp', split_axis=0, concat_axis=1, tiled=True)]
    all_to_all x1, starting transfers between devices: 3.47 us -> 6.52 us  [mod_back(): lax.all_to_all(embed_terms, 'dp', split_axis=0, concat_axis=1, tiled=True)]
  transfers between devices with their start and end apart: 38 -> 38, of which waited for: 19 -> 18; matrix products, arithmetic and copies ran while one was open for 4% -> 4% of each run, Pallas kernels for 27% -> 28%
where the time goes in v2:
time: 255 us; the launch traced here: 253 us
  Pallas kernels  108 us (42%)
  waiting for transfers between devices  77.4 us (30%)
  starting transfers between devices  47.9 us (19%)
  local copies, waits for them, and re-layouts  9.67 us (4%)
  other arithmetic  6.44 us (3%)
    pallas_call x39, Pallas kernels, call(): pl.pallas_call(wrapped, grid=grid, in_specs=in_specs, out_specs=out_specs...  108 us
    ppermute x25, waiting for transfers between devices, bit_swap(): return lax.ppermute(value, ('dp', 'tensor'), pairs)  57.7 us
    ppermute x25, starting transfers between devices, bit_swap(): return lax.ppermute(value, ('dp', 'tensor'), pairs)  27.1 us
    all_to_all x1, starting transfers between devices, shards(): lax.all_to_all(temb, 'dp', split_axis=1, concat_axis=0, tiled=True)  8.31 us
    all_to_all x1, waiting for transfers between devices, shards(): lax.all_to_all(temb, 'dp', split_axis=1, concat_axis=0, tiled=True)  7.18 us
    all_to_all x1, starting transfers between devices, mod_back(): lax.all_to_all(embed_terms, 'dp', split_axis=0, concat_axis=1, tiled=True)  6.52 us
    all_to_all x1, waiting for transfers between devices, shards(): lax.all_to_all(mod_terms, 'dp', split_axis=0, concat_axis=0, tiled=True)  5.16 us
  transfers between devices with their start and end apart: 38, of which 18 were waited for; matrix products, arithmetic and copies ran while one was open for 4% of the time, Pallas kernels for 28%

profile of v2, /device:TPU:0, one launch (start us, length us, event | category | flops | bytes accessed | tf_op | source)
XLA Modules:
  0.0 253.4 jit_solution(14468495967946303470)
XLA Ops:
  2.2 8.3 %all-to-all-start = ((bf16[1,16,48]{2,0,1:T(2,128)(2,1)}), bf16[1,16,48]{2,0,1:T(2,128)(2,1)S(1)}, u32[]{:S(2)}, u32[]{:S(2)}) async-start(bf16[1,16,48]{2,0,1:T(2,128)(2,1)} %all_to_all.38), calls=%async_computation | async-start | bytes 16384 | tf_op jit(solution)/shard_map/all_to_all | solution.py:1005
  10.5 7.2 %all-to-all-done = bf16[1,16,48]{2,0,1:T(2,128)(2,1)S(1)} async-done(((bf16[1,16,48]{2,0,1:T(2,128)(2,1)}), bf16[1,16,48]{2,0,1:T(2,128)(2,1)S(1)}, u32[]{:S(2)}, u32[]{:S(2)}) %all-to-all-start) | async-done | bytes 1568 | tf_op jit(solution)/shard_map/all_to_all | solution.py:1005
  18.9 3.5 %all-to-all-start.1 = ((f32[16,1,4608]{2,1,0:T(1,128)}), f32[16,1,4608]{2,1,0:T(1,128)S(1)}, u32[]{:S(2)}, u32[]{:S(2)}) async-start(f32[16,1,4608]{2,1,0:T(1,128)} %copy.34), calls=%async_computation.1 | async-start | bytes 589824 | tf_op jit(solution)/shard_map/all_to_all | solution.py:1014
  23.2 3.1 %fusion.3 = (f32[1024,128]{1,0:T(8,128)}, f32[1024,128]{1,0:T(8,128)}) fusion(f32[128]{0:T(128)S(1)} %get-tuple-element.290, f32[128]{0:T(128)S(1)} %get-tuple-element.291, f32[1024]{0:T(1024)S(1)} %add_convert_fusion), kind=kLoop, calls=%fused_computation.10 | loop fusion | flops 262144 | bytes 1053696 | tf_op jit(solution)/shard_map/mul | solution.py:407
  26.6 5.2 %all-to-all-done.1 = f32[16,1,4608]{2,1,0:T(1,128)S(1)} async-done(((f32[16,1,4608]{2,1,0:T(1,128)}), f32[16,1,4608]{2,1,0:T(1,128)S(1)}, u32[]{:S(2)}, u32[]{:S(2)}) %all-to-all-start.1) | async-done | bytes 294944 | tf_op jit(solution)/shard_map/all_to_all | solution.py:1014
  35.9 22.4 %shard_map.255 = (bf16[3,2,2,1024,512]{4,3,2,1,0:T(8,128)(2,1)}, bf16[384,1024]{1,0:T(8,128)(2,1)}, f32[3,2,1,1024]{3,2,1,0:T(1,128)S(1)}, f32[512,768]{1,0:T(8,...) custom-call(s32[2]{0:T(128)S(1)} %add_clamp_fusion.refs_0_, ...), custom_call_target="tpu_custom_call" | custom-call | tf_op jit(solution)/shard_map/pallas_call | solution.py:122
  62.2 2.4 shard_map.258
  64.6 8.4 %shard_map.259 = (bf16[768,768]{1,0:T(8,128)(2,1)}, bf16[768,768]{1,0:T(8,128)(2,1)}, f32[1,768]{1,0:T(1,128)S(1)}, bf16[1024,768]{1,0:T(8,128)(2,1)S(1)}, bf16[...) custom-call(s32[1]{0:T(128)} %bitcast.7.refs_0_, bf16[512,768]{1,0:T(8,128)(2,1)S(1)} %get-tuple-element.161.refs_0_.refs_1_, ...), custom_call_target="tpu_custom_call" | custom-call | tf_op jit(solution)/shard_map/pallas_call | solution.py:122
  73.1 13.7 %shard_map.260 = (bf16[768,768]{1,0:T(8,128)(2,1)}, bf16[768,768]{1,0:T(8,128)(2,1)}, f32[1,768]{1,0:T(1,128)S(1)}, f32[512,768]{1,0:T(8,128)S(1)}, bf16[512,768...) custom-call(s32[1]{0:T(128)} %bitcast.7.refs_0_, ...), custom_call_target="tpu_custom_call" | custom-call | tf_op jit(solution)/shard_map/pallas_call | solution.py:122
  91.2 3.1 %mlp_first.6 = (bf16[384,768]{1,0:T(8,128)(2,1)}, bf16[384,768]{1,0:T(8,128)(2,1)S(1)}, f32[8,128]{1,0:T(8,128)S(1)}) custom-call(s32[1]{0:T(128)} %bitcast.9.refs_0_, bf16[768,768]{1,0:T(8,128)(2,1)S(1)} %copy-done.11, bf16[768,768]{1,0:T(8,128)(2,1)} %collective-permute-done.5.refs_2_, f32[8,128]{1,0:T(8,128)S(1)} %get-tuple-element.173.refs_3_), custom_call_target="tpu_custom_call" | custom-call | flops 1000000000 | tf_op jit(solution)/shard_map/mlp_first/pallas_call | solution.py:122
  94.3 3.6 %turn.1 = (f32[512,768]{1,0:T(8,128)}, bf16[512,768]{1,0:T(8,128)(2,1)}, f32[8,768]{1,0:T(8,128)S(1)}, f32[8,128]{1,0:T(8,128)S(1)}) custom-call(s32[2]{0:T(128)S(1)} %add_clamp_fusion.refs_0_, bf16[512,768]{1,0:T(8,128)(2,1)S(1)} %bitcast.51, bf16[512,768]{1,0:T(8,128)(2,1)S(1)} %bitcast.57, f32[512,768]{1,0:T(8,128)S(1)} %copy-done.4, ...), custom_call_target="tpu_custom_call" | custom-call | flops 1000000000 | tf_op jit(solution)/shard_map/turn/pallas_call | solution.py:122
  101.6 24.5 %back.1 = (bf16[768,768]{1,0:T(8,128)(2,1)S(1)}, bf16[768,768]{1,0:T(8,128)(2,1)S(1)}, f32[3,384]{1,0:T(4,128)S(1)}, bf16[1024,384]{1,0:T(8,128)(2,1)S(1)}, bf16...) custom-call(s32[1]{0:T(128)} %bitcast.7.refs_0_, ...), custom_call_target="tpu_custom_call" | custom-call | flops 1000000000 | tf_op jit(solution)/shard_map/back/pallas_call | solution.py:122
  132.0 2.7 %d_attn_in.1 = (f32[512,768]{1,0:T(8,128)S(1)}, bf16[512,768]{1,0:T(8,128)(2,1)S(1)}, f32[8,128]{1,0:T(8,128)S(1)}) custom-call(bf16[1024,384]{1,0:T(8,128)(2,1)S(1)} %get-tuple-element.196.refs_0_, bf16[1024,384]{1,0:T(8,128)(2,1)S(1)} %get-tuple-element.197.refs_1_, bf16[1024,384]{1,0:T(8,128)(2,1)S(1)} %get-tuple-element.198.refs_2_, ...), custom_call_target="tpu_custom_call" | custom-call | flops 1000000000 | tf_op jit(solution)/shard_map/d_attn_in/pallas_call | solution.py:122
  135.2 9.2 %collective-permute-done.12.refs_2_ = bf16[384,768]{1,0:T(8,128)(2,1)S(1)} collective-permute-done((bf16[384,768]{1,0:T(8,128)(2,1)S(1)}, bf16[384,768]{1,0:T(8,128)(2,1)S(1)}, u32[]{:S(2)}, u32[]{:S(2)}) %collective-permute-start.12) | collective-permute-done | bytes 589856 | tf_op jit(solution)/shard_map/mlp_second/ppermute | solution.py:670
  147.2 2.2 finish.1
  149.3 2.2 end.1
  151.6 4.3 %collective-permute-done.16.refs_1_ = bf16[192,768]{1,0:T(8,128)(2,1)S(1)} collective-permute-done((bf16[192,768]{1,0:T(8,128)(2,1)S(1)}, bf16[192,768]{1,0:T(8,128)(2,1)S(1)}, u32[]{:S(2)}, u32[]{:S(2)}) %collective-permute-start.16) | collective-permute-done | bytes 294944 | tf_op jit(solution)/shard_map/mlp_second/ppermute | solution.py:670
  156.5 2.2 collective-permute-start.17
  160.5 6.2 %collective-permute-done.17.refs_2_ = bf16[384,768]{1,0:T(8,128)(2,1)S(1)} collective-permute-done((bf16[384,768]{1,0:T(8,128)(2,1)S(1)}, bf16[384,768]{1,0:T(8,128)(2,1)S(1)}, u32[]{:S(2)}, u32[]{:S(2)}) %collective-permute-start.17) | collective-permute-done | bytes 589856 | tf_op jit(solution)/shard_map/projections/ppermute | solution.py:670
  172.6 8.8 %collective-permute-done.21.refs_1_ = bf16[192,768]{1,0:T(8,128)(2,1)S(1)} collective-permute-done((bf16[192,768]{1,0:T(8,128)(2,1)S(1)}, bf16[192,768]{1,0:T(8,128)(2,1)S(1)}, u32[]{:S(2)}, u32[]{:S(2)}) %collective-permute-start.21) | collective-permute-done | bytes 294944 | tf_op jit(solution)/shard_map/mlp_second/ppermute | solution.py:670
  184.7 2.7 %collective-permute-start.27 = (bf16[192,768]{1,0:T(8,128)(2,1)S(1)}, bf16[192,768]{1,0:T(8,128)(2,1)S(1)}, u32[]{:S(2)}, u32[]{:S(2)}) collective-permute-start(bf16[192,768]{1,0:T(8,128)(2,1)S(1)} %get-tuple-element.246.refs_1_), channel_id=1, source_target_pairs={{0,8},{1,9},{2,10},{3,11},{4,12},{5,13},{6,14},{7,15},{8,0},{9,1},... | collective-permute-start | bytes 884744 | tf_op jit(solution)/shard_map/mlp_second/ppermute | solution.py:670
  188.3 9.3 %collective-permute-done.24.refs_1_ = bf16[192,768]{1,0:T(8,128)(2,1)S(1)} collective-permute-done((bf16[192,768]{1,0:T(8,128)(2,1)S(1)}, bf16[192,768]{1,0:T(8,128)(2,1)S(1)}, u32[]{:S(2)}, u32[]{:S(2)}) %collective-permute-start.24) | collective-permute-done | bytes 294944 | tf_op jit(solution)/shard_map/projections/ppermute | solution.py:670
  198.6 2.5 unpack_first.1
  201.1 6.5 %collective-permute-done.29.refs_2_ = bf16[192,768]{1,0:T(8,128)(2,1)S(1)} collective-permute-done((bf16[192,768]{1,0:T(8,128)(2,1)S(1)}, bf16[192,768]{1,0:T(8,128)(2,1)S(1)}, u32[]{:S(2)}, u32[]{:S(2)}) %collective-permute-start.29) | collective-permute-done | bytes 294944 | tf_op jit(solution)/shard_map/projections/ppermute | solution.py:670
  210.7 4.6 %collective-permute-done.26.refs_1_ = bf16[64,768]{1,0:T(8,128)(2,1)S(1)} collective-permute-done((bf16[64,768]{1,0:T(8,128)(2,1)S(1)}, bf16[64,768]{1,0:T(8,128)(2,1)S(1)}, u32[]{:S(2)}, u32[]{:S(2)}) %collective-permute-start.26) | collective-permute-done | bytes 98336 | tf_op jit(solution)/shard_map/small/ppermute | solution.py:670
  216.0 2.2 collective-permute-start.31
  218.7 7.0 %collective-permute-done.32.refs_2_ = bf16[384,768]{1,0:T(8,128)(2,1)} collective-permute-done((bf16[384,768]{1,0:T(8,128)(2,1)S(1)}, bf16[384,768]{1,0:T(8,128)(2,1)}, u32[]{:S(2)}, u32[]{:S(2)}) %collective-permute-start.32) | collective-permute-done | bytes 589856 | tf_op jit(solution)/shard_map/projections/ppermute | solution.py:670
  225.7 2.2 projections.11
  229.5 2.5 unpack_second.1
  233.5 6.5 %all-to-all-start.2 = ((f32[16,1,48]{2,1,0:T(1,128)}), f32[16,1,48]{2,1,0:T(1,128)S(1)}, u32[]{:S(2)}, u32[]{:S(2)}) async-start(f32[16,1,48]{2,1,0:T(1,128)} %bitcast.15), calls=%async_computation.2 | async-start | bytes 16384 | tf_op jit(solution)/shard_map/mod_back/all_to_all | solution.py:1109
  244.0 3.2 %all-to-all-done.2 = f32[16,1,48]{2,1,0:T(1,128)S(1)} async-done(((f32[16,1,48]{2,1,0:T(1,128)}), f32[16,1,48]{2,1,0:T(1,128)S(1)}, u32[]{:S(2)}, u32[]{:S(2)}) %all-to-all-start.2) | async-done | bytes 3104 | tf_op jit(solution)/shard_map/mod_back/all_to_all | solution.py:1109
  249.1 4.1 %shard_map.261 = (f32[3,768,384]{2,1,0:T(8,128)}, f32[384,768]{1,0:T(8,128)}, f32[8,128]{1,0:T(8,128)}) custom-call(s32[1]{0:T(128)} %bitcast.7.refs_0_, bf16[768,768]{1,0:T(8,128)(2,1)} %get-tuple-element.266.refs_1_, bf16[768,768]{1,0:T(8,128)(2,1)} %collective-permute-done.34.refs_2_, f32[8,128]{1,0:T(8,128)S(1)} %get-tuple-element.267.refs_3_), custom_call_target="tpu_custom_call" | custom-call | flops 1000000000 | tf_op jit(solution)/shard_map/pallas_call | solution.py:122
  (184 shorter events, 54.8 us)
Async XLA Ops:
  2.2 15.5 %all-to-all-start = ((bf16[1,16,48]{2,0,1:T(2,128)(2,1)}), bf16[1,16,48]{2,0,1:T(2,128)(2,1)S(1)}, u32[]{:S(2)}, u32[]{:S(2)}) async-start(bf16[1,16,48]{2,0,1:T(2,128)(2,1)} %all_to_all.38), calls=%async_computation | async-start | bytes 16384 | tf_op jit(solution)/shard_map/all_to_all | solution.py:1005
  18.9 12.8 %all-to-all-start.1 = ((f32[16,1,4608]{2,1,0:T(1,128)}), f32[16,1,4608]{2,1,0:T(1,128)S(1)}, u32[]{:S(2)}, u32[]{:S(2)}) async-start(f32[16,1,4608]{2,1,0:T(1,128)} %copy.34), calls=%async_computation.1 | async-start | bytes 589824 | tf_op jit(solution)/shard_map/all_to_all | solution.py:1014
  73.1 16.8 %collective-permute-start.5 = (bf16[768,768]{1,0:T(8,128)(2,1)}, bf16[768,768]{1,0:T(8,128)(2,1)}, u32[]{:S(2)}, u32[]{:S(2)}) collective-permute-start(bf16[768,768]{1,0:T(8,128)(2,1)} %get-tuple-element.172), channel_id=1, source_target_pairs={{0,2},{1,5},{2,0},{3,7},{4,6},{5,1},{6,4},{7,3},{8,10},{9,13},{10,... | collective-permute-start | bytes 3538952 | tf_op jit(solution)/shard_map/mlp_first/ppermute | solution.py:670
  87.9 6.4 %collective-permute-start.8 = (bf16[512,768]{1,0:T(8,128)(2,1)}, bf16[512,768]{1,0:T(8,128)(2,1)S(1)}, u32[]{:S(2)}, u32[]{:S(2)}) collective-permute-start(bf16[512,768]{1,0:T(8,128)(2,1)} %get-tuple-element.179), channel_id=1, source_target_pairs={{0,1},{1,0},{2,3},{3,2},{4,5},{5,4},{6,7},{7,6},{8,9},{9,8},{10,11... | collective-permute-start | bytes 2359304 | tf_op jit(solution)/shard_map/ppermute | solution.py:661
  89.0 37.2 %collective-permute-start.7 = (bf16[768,768]{1,0:T(8,128)(2,1)}, bf16[768,768]{1,0:T(8,128)(2,1)}, u32[]{:S(2)}, u32[]{:S(2)}) collective-permute-start(bf16[768,768]{1,0:T(8,128)(2,1)} %get-tuple-element.177), channel_id=1, source_target_pairs={{0,2},{1,5},{2,0},{3,7},{4,6},{5,1},{6,4},{7,3},{8,10},{9,13},{10,... | collective-permute-start | bytes 3538952 | tf_op jit(solution)/shard_map/mlp_second/ppermute | solution.py:670
  98.3 32.0 %collective-permute-start.6 = (bf16[384,768]{1,0:T(8,128)(2,1)}, bf16[384,768]{1,0:T(8,128)(2,1)}, u32[]{:S(2)}, u32[]{:S(2)}) collective-permute-start(bf16[384,768]{1,0:T(8,128)(2,1)} %get-tuple-element.175), channel_id=1, source_target_pairs={{0,4},{1,3},{2,6},{3,1},{4,0},{5,7},{6,2},{7,5},{8,12},{9,11},{10,... | collective-permute-start | bytes 1769480 | tf_op jit(solution)/shard_map/mlp_first/ppermute | solution.py:670
  99.3 47.6 %collective-permute-start.4 = (bf16[512,768]{1,0:T(8,128)(2,1)}, bf16[512,768]{1,0:T(8,128)(2,1)S(1)}, u32[]{:S(2)}, u32[]{:S(2)}) collective-permute-start(bf16[512,768]{1,0:T(8,128)(2,1)} %get-tuple-element.170), channel_id=1, source_target_pairs={{0,1},{1,0},{2,3},{3,2},{4,5},{5,4},{6,7},{7,6},{8,9},{9,8},{10,11... | collective-permute-start | bytes 2359304 | tf_op jit(solution)/shard_map/ppermute | solution.py:661
  128.1 16.3 %collective-permute-start.12 = (bf16[384,768]{1,0:T(8,128)(2,1)S(1)}, bf16[384,768]{1,0:T(8,128)(2,1)S(1)}, u32[]{:S(2)}, u32[]{:S(2)}) collective-permute-start(bf16[384,768]{1,0:T(8,128)(2,1)S(1)} %get-tuple-element.195), channel_id=1, source_target_pairs={{0,4},{1,3},{2,6},{3,1},{4,0},{5,7},{6,2},{7,5},{8,12},{9,11},{10,... | collective-permute-start | bytes 1769480 | tf_op jit(solution)/shard_map/mlp_second/ppermute | solution.py:670
  129.2 26.7 %collective-permute-start.15 = (bf16[768,768]{1,0:T(8,128)(2,1)S(1)}, bf16[768,768]{1,0:T(8,128)(2,1)S(1)}, u32[]{:S(2)}, u32[]{:S(2)}) collective-permute-start(bf16[768,768]{1,0:T(8,128)(2,1)S(1)} %get-tuple-element.219), channel_id=1, source_target_pairs={{0,2},{1,5},{2,0},{3,7},{4,6},{5,1},{6,4},{7,3},{8,10},{9,13},{10,... | collective-permute-start | bytes 3538952 | tf_op jit(solution)/shard_map/back/projections/ppermute | solution.py:670
  134.6 14.7 %collective-permute-start.13 = (bf16[512,768]{1,0:T(8,128)(2,1)S(1)}, bf16[512,768]{1,0:T(8,128)(2,1)S(1)}, u32[]{:S(2)}, u32[]{:S(2)}) collective-permute-start(bf16[512,768]{1,0:T(8,128)(2,1)S(1)} %get-tuple-element.206), channel_id=1, source_target_pairs={{0,1},{1,0},{2,3},{3,2},{4,5},{5,4},{6,7},{7,6},{8,9},{9,8},{10,11... | collective-permute-start | bytes 2359304 | tf_op jit(solution)/shard_map/d_attn_in/ppermute | solution.py:661
  134.7 10.5 %collective-permute-start.11 = (bf16[192,768]{1,0:T(8,128)(2,1)S(1)}, bf16[192,768]{1,0:T(8,128)(2,1)S(1)}, u32[]{:S(2)}, u32[]{:S(2)}) collective-permute-start(bf16[192,768]{1,0:T(8,128)(2,1)S(1)} %get-tuple-element.193), channel_id=1, source_target_pairs={{0,8},{1,9},{2,10},{3,11},{4,12},{5,13},{6,14},{7,15},{8,0},{9,1},... | collective-permute-start | bytes 884744 | tf_op jit(solution)/shard_map/mlp_first/ppermute | solution.py:670
  144.7 11.1 %collective-permute-start.16 = (bf16[192,768]{1,0:T(8,128)(2,1)S(1)}, bf16[192,768]{1,0:T(8,128)(2,1)S(1)}, u32[]{:S(2)}, u32[]{:S(2)}) collective-permute-start(bf16[192,768]{1,0:T(8,128)(2,1)S(1)} %get-tuple-element.221), channel_id=1, source_target_pairs={{0,8},{1,9},{2,10},{3,11},{4,12},{5,13},{6,14},{7,15},{8,0},{9,1},... | collective-permute-start | bytes 884744 | tf_op jit(solution)/shard_map/mlp_second/ppermute | solution.py:670
  145.4 14.9 %collective-permute-start.18 = (bf16[192,768]{1,0:T(8,128)(2,1)S(1)}, bf16[192,768]{1,0:T(8,128)(2,1)S(1)}, u32[]{:S(2)}, u32[]{:S(2)}) collective-permute-start(bf16[192,768]{1,0:T(8,128)(2,1)S(1)} %get-tuple-element.226.refs_0_), channel_id=1, source_target_pairs={{0,16},{1,17},{2,18},{3,19},{4,20},{5,21},{6,22},{7,23},{8,24},{9,... | collective-permute-start | bytes 884744 | tf_op jit(solution)/shard_map/mlp_first/ppermute | solution.py:670
  156.5 10.1 %collective-permute-start.17 = (bf16[384,768]{1,0:T(8,128)(2,1)S(1)}, bf16[384,768]{1,0:T(8,128)(2,1)S(1)}, u32[]{:S(2)}, u32[]{:S(2)}) collective-permute-start(bf16[384,768]{1,0:T(8,128)(2,1)S(1)} %get-tuple-element.225), channel_id=1, source_target_pairs={{0,4},{1,3},{2,6},{3,1},{4,0},{5,7},{6,2},{7,5},{8,12},{9,11},{10,... | collective-permute-start | bytes 1769480 | tf_op jit(solution)/shard_map/projections/ppermute | solution.py:670
  160.3 6.8 %collective-permute-start.22 = (bf16[192,768]{1,0:T(8,128)(2,1)S(1)}, bf16[192,768]{1,0:T(8,128)(2,1)S(1)}, u32[]{:S(2)}, u32[]{:S(2)}) collective-permute-start(bf16[192,768]{1,0:T(8,128)(2,1)S(1)} %get-tuple-element.234.refs_1_), channel_id=1, source_target_pairs={{0,8},{1,9},{2,10},{3,11},{4,12},{5,13},{6,14},{7,15},{8,0},{9,1},... | collective-permute-start | bytes 884744 | tf_op jit(solution)/shard_map/mlp_first/ppermute | solution.py:670
  160.4 6.6 %collective-permute-start.14 = (f32[16,768]{1,0:T(8,128)S(1)}, f32[16,768]{1,0:T(8,128)S(1)}, u32[]{:S(2)}, u32[]{:S(2)}) collective-permute-start(f32[16,768]{1,0:T(8,128)S(1)} %get-tuple-element.214.refs_0_), channel_id=1, source_target_pairs={{0,1},{1,0},{2,3},{3,2},{4,5},{5,4},{6,7},{7,6},{8,9},{9,8},{10,11... | collective-permute-start | bytes 147464 | tf_op jit(solution)/shard_map/share/ppermute | solution.py:661
  167.1 14.7 %collective-permute-start.25 = (bf16[384,768]{1,0:T(8,128)(2,1)S(1)}, bf16[384,768]{1,0:T(8,128)(2,1)S(1)}, u32[]{:S(2)}, u32[]{:S(2)}) collective-permute-start(bf16[384,768]{1,0:T(8,128)(2,1)S(1)} %get-tuple-element.241.refs_1_), channel_id=1, source_target_pairs={{0,4},{1,3},{2,6},{3,1},{4,0},{5,7},{6,2},{7,5},{8,12},{9,11},{10,... | collective-permute-start | bytes 1769480 | tf_op jit(solution)/shard_map/mlp_first/ppermute | solution.py:670
  169.1 12.2 %collective-permute-start.21 = (bf16[192,768]{1,0:T(8,128)(2,1)S(1)}, bf16[192,768]{1,0:T(8,128)(2,1)S(1)}, u32[]{:S(2)}, u32[]{:S(2)}) collective-permute-start(bf16[192,768]{1,0:T(8,128)(2,1)S(1)} %get-tuple-element.233.refs_0_), channel_id=1, source_target_pairs={{0,16},{1,17},{2,18},{3,19},{4,20},{5,21},{6,22},{7,23},{8,24},{9,... | collective-permute-start | bytes 884744 | tf_op jit(solution)/shard_map/mlp_second/ppermute | solution.py:670
  170.6 11.1 %collective-permute-start.20 = (bf16[192,768]{1,0:T(8,128)(2,1)S(1)}, bf16[192,768]{1,0:T(8,128)(2,1)S(1)}, u32[]{:S(2)}, u32[]{:S(2)}) collective-permute-start(bf16[192,768]{1,0:T(8,128)(2,1)S(1)} %get-tuple-element.232), channel_id=1, source_target_pairs={{0,8},{1,9},{2,10},{3,11},{4,12},{5,13},{6,14},{7,15},{8,0},{9,1},... | collective-permute-start | bytes 884744 | tf_op jit(solution)/shard_map/projections/ppermute | solution.py:670
  172.3 9.5 %collective-permute-start.19 = (bf16[16,768]{1,0:T(8,128)(2,1)S(1)}, bf16[16,768]{1,0:T(8,128)(2,1)S(1)}, u32[]{:S(2)}, u32[]{:S(2)}) collective-permute-start(bf16[16,768]{1,0:T(8,128)(2,1)S(1)} %get-tuple-element.230.refs_0_), channel_id=1, source_target_pairs={{0,2},{1,3},{2,0},{3,1},{4,6},{5,7},{6,4},{7,5},{8,10},{9,11},{10,... | collective-permute-start | bytes 73736 | tf_op jit(solution)/shard_map/begin/ppermute | solution.py:670
  181.9 16.7 %collective-permute-start.30 = (bf16[768,768]{1,0:T(8,128)(2,1)S(1)}, bf16[768,768]{1,0:T(8,128)(2,1)S(1)}, u32[]{:S(2)}, u32[]{:S(2)}) collective-permute-start(bf16[768,768]{1,0:T(8,128)(2,1)S(1)} %get-tuple-element.250.refs_1_), channel_id=1, source_target_pairs={{0,2},{1,5},{2,0},{3,7},{4,6},{5,1},{6,4},{7,3},{8,10},{9,13},{10,... | collective-permute-start | bytes 3538952 | tf_op jit(solution)/shard_map/mlp_first/ppermute | solution.py:670
  183.7 13.9 %collective-permute-start.24 = (bf16[192,768]{1,0:T(8,128)(2,1)S(1)}, bf16[192,768]{1,0:T(8,128)(2,1)S(1)}, u32[]{:S(2)}, u32[]{:S(2)}) collective-permute-start(bf16[192,768]{1,0:T(8,128)(2,1)S(1)} %get-tuple-element.240.refs_0_), channel_id=1, source_target_pairs={{0,16},{1,17},{2,18},{3,19},{4,20},{5,21},{6,22},{7,23},{8,24},{9,... | collective-permute-start | bytes 884744 | tf_op jit(solution)/shard_map/projections/ppermute | solution.py:670
  184.7 13.0 %collective-permute-start.27 = (bf16[192,768]{1,0:T(8,128)(2,1)S(1)}, bf16[192,768]{1,0:T(8,128)(2,1)S(1)}, u32[]{:S(2)}, u32[]{:S(2)}) collective-permute-start(bf16[192,768]{1,0:T(8,128)(2,1)S(1)} %get-tuple-element.246.refs_1_), channel_id=1, source_target_pairs={{0,8},{1,9},{2,10},{3,11},{4,12},{5,13},{6,14},{7,15},{8,0},{9,1},... | collective-permute-start | bytes 884744 | tf_op jit(solution)/shard_map/mlp_second/ppermute | solution.py:670
  187.4 10.3 %collective-permute-start.23 = (bf16[32,768]{1,0:T(8,128)(2,1)S(1)}, bf16[32,768]{1,0:T(8,128)(2,1)S(1)}, u32[]{:S(2)}, u32[]{:S(2)}) collective-permute-start(bf16[32,768]{1,0:T(8,128)(2,1)S(1)} %get-tuple-element.239.refs_0_), channel_id=1, source_target_pairs={{0,4},{1,5},{2,6},{3,7},{4,0},{5,1},{6,2},{7,3},{8,12},{9,13},{10,... | collective-permute-start | bytes 147464 | tf_op jit(solution)/shard_map/small/ppermute | solution.py:670
  197.7 9.9 %collective-permute-start.28 = (bf16[384,768]{1,0:T(8,128)(2,1)S(1)}, bf16[384,768]{1,0:T(8,128)(2,1)S(1)}, u32[]{:S(2)}, u32[]{:S(2)}) collective-permute-start(bf16[384,768]{1,0:T(8,128)(2,1)S(1)} %get-tuple-element.248.refs_1_), channel_id=1, source_target_pairs={{0,4},{1,3},{2,6},{3,1},{4,0},{5,7},{6,2},{7,5},{8,12},{9,11},{10,... | collective-permute-start | bytes 1769480 | tf_op jit(solution)/shard_map/mlp_second/ppermute | solution.py:670
  198.2 9.4 %collective-permute-start.29 = (bf16[192,768]{1,0:T(8,128)(2,1)S(1)}, bf16[192,768]{1,0:T(8,128)(2,1)S(1)}, u32[]{:S(2)}, u32[]{:S(2)}) collective-permute-start(bf16[192,768]{1,0:T(8,128)(2,1)S(1)} %get-tuple-element.249.refs_1_), channel_id=1, source_target_pairs={{0,8},{1,9},{2,10},{3,11},{4,12},{5,13},{6,14},{7,15},{8,0},{9,1},... | collective-permute-start | bytes 884744 | tf_op jit(solution)/shard_map/projections/ppermute | solution.py:670
  207.8 21.7 %collective-permute-start.33 = (bf16[768,768]{1,0:T(8,128)(2,1)S(1)}, bf16[768,768]{1,0:T(8,128)(2,1)S(1)}, u32[]{:S(2)}, u32[]{:S(2)}) collective-permute-start(bf16[768,768]{1,0:T(8,128)(2,1)S(1)} %get-tuple-element.260.refs_1_), channel_id=1, source_target_pairs={{0,2},{1,5},{2,0},{3,7},{4,6},{5,1},{6,4},{7,3},{8,10},{9,13},{10,... | collective-permute-start | bytes 3538952 | tf_op jit(solution)/shard_map/mlp_second/ppermute | solution.py:670
  209.3 16.4 %collective-permute-start.32 = (bf16[384,768]{1,0:T(8,128)(2,1)S(1)}, bf16[384,768]{1,0:T(8,128)(2,1)}, u32[]{:S(2)}, u32[]{:S(2)}) collective-permute-start(bf16[384,768]{1,0:T(8,128)(2,1)S(1)} %get-tuple-element.256.refs_1_), channel_id=1, source_target_pairs={{0,4},{1,3},{2,6},{3,1},{4,0},{5,7},{6,2},{7,5},{8,12},{9,11},{10,... | collective-permute-start | bytes 1769480 | tf_op jit(solution)/shard_map/projections/ppermute | solution.py:670
  210.7 4.6 %collective-permute-start.26 = (bf16[64,768]{1,0:T(8,128)(2,1)S(1)}, bf16[64,768]{1,0:T(8,128)(2,1)S(1)}, u32[]{:S(2)}, u32[]{:S(2)}) collective-permute-start(bf16[64,768]{1,0:T(8,128)(2,1)S(1)} %get-tuple-element.245.refs_0_), channel_id=1, source_target_pairs={{0,8},{1,9},{2,10},{3,11},{4,12},{5,13},{6,14},{7,15},{8,0},{9,1},... | collective-permute-start | bytes 294920 | tf_op jit(solution)/shard_map/small/ppermute | solution.py:670
  216.0 12.5 %collective-permute-start.31 = (bf16[128,768]{1,0:T(8,128)(2,1)}, bf16[128,768]{1,0:T(8,128)(2,1)}, u32[]{:S(2)}, u32[]{:S(2)}) collective-permute-start(bf16[128,768]{1,0:T(8,128)(2,1)} %get-tuple-element.255.refs_0_), channel_id=1, source_target_pairs={{0,16},{1,17},{2,18},{3,19},{4,20},{5,21},{6,22},{7,23},{8,24},{9,... | collective-permute-start | bytes 589832 | tf_op jit(solution)/shard_map/small/ppermute | solution.py:670
  227.9 21.2 %collective-permute-start.34 = (bf16[768,768]{1,0:T(8,128)(2,1)}, bf16[768,768]{1,0:T(8,128)(2,1)}, u32[]{:S(2)}, u32[]{:S(2)}) collective-permute-start(bf16[768,768]{1,0:T(8,128)(2,1)} %get-tuple-element.266.refs_1_), channel_id=1, source_target_pairs={{0,2},{1,5},{2,0},{3,7},{4,6},{5,1},{6,4},{7,3},{8,10},{9,13},{10,... | collective-permute-start | bytes 3538952 | tf_op jit(solution)/shard_map/projections/ppermute | solution.py:670
  233.5 13.7 %all-to-all-start.2 = ((f32[16,1,48]{2,1,0:T(1,128)}), f32[16,1,48]{2,1,0:T(1,128)S(1)}, u32[]{:S(2)}, u32[]{:S(2)}) async-start(f32[16,1,48]{2,1,0:T(1,128)} %bitcast.15), calls=%async_computation.2 | async-start | bytes 16384 | tf_op jit(solution)/shard_map/mod_back/all_to_all | solution.py:1109
  (26 other events, 159.6 us)
